TPU v7x, 128 devices: a whole 4x4x4 slice. The times are simulated.
128 devices in a mesh: seq: 8 (over y_hi, z), fsdp: 16 (over y_lo, x, core).
Axes of the slice: x: 4, y: 4 (y_hi: 2, y_lo: 2; y = y_hi * 2 + y_lo), z: 4, core: 2. Of those that a mesh axis runs over, the one named last changes fastest.
Arguments:
- signal: bfloat16 [16, 1024, 8192], P('fsdp', 'seq'), may hold values from -6 to 6
- gating: bfloat16 [16, 1024, 8192], P('fsdp', 'seq'), may hold values from -6 to 6
- low_rank: bfloat16 [16, 1024, 512], P('fsdp', 'seq'), may hold values from -6 to 6
- dt_weight: bfloat16 [512, 8192], P(None, 'fsdp'), may hold values from -0.25 to 0.25
- dt_bias: float32 [8192], P('fsdp'), may hold values from -1 to 0.5
- decay_rate: float32 [16, 8192], P(None, 'fsdp'), may hold values from 0 to 0.05, as said below
- skip_gain: float32 [8192], P('fsdp'), may hold values from 0.5 to 1.5
- coef_in: float32 [16, 16, 1024], P('fsdp', None, 'seq'), may hold values from -4 to 4
- coef_out: float32 [16, 16, 1024], P('fsdp', None, 'seq'), may hold values from -0.1875 to 0.1875
- segment_ids: int32 [16, 1024], P('fsdp', 'seq'), may hold values from 0 to 3, never falling along the last dimension, each value on 1 to 512 neighbouring positions
- out_grad: bfloat16 [16, 1024, 8192], P('fsdp', 'seq'), may hold values from -6 to 6
Outputs:
- grad_signal: bfloat16 [16, 1024, 8192], P('fsdp', 'seq')
- grad_gating: bfloat16 [16, 1024, 8192], P('fsdp', 'seq')
- grad_low_rank: float32 [16, 1024, 512], P('fsdp', 'seq')
- grad_coef_in: float32 [16, 16, 1024], P('fsdp', None, 'seq')
- grad_coef_out: float32 [16, 16, 1024], P('fsdp', None, 'seq')
- grad_dt_weight: float32 [512, 8192], P(None, 'fsdp')
- grad_rate: float32 [16, 8192], P(None, 'fsdp')
- grad_skip: float32 [8192], P('fsdp')
- grad_bias: float32 [8192], P('fsdp')
Inputs may be any that keep to these rules, and one draw needn't show every extreme that they name: `segment_ids`: segment numbers never fall along a sequence; each document is a run of one number. `decay_rate`: positive rates.
All inputs are finite; a program needn't handle non-finite values.
Results may differ from a plain program's by a relative error of at most 0.0029.
Values may be sent and summed in bfloat16 or wider, within the bound.
A program may use at most 192 MiB of HBM per device.

v0:
```python
import jax
import jax.numpy as jnp
from jax import lax
from jax.sharding import PartitionSpec as P

step_block = 16


def from_behind(x, axis, by):
    devices = lax.axis_size(axis)
    pairs = [(i, i + by) for i in range(devices) if 0 <= i + by < devices]
    return lax.ppermute(x, axis, pairs)


def shards(
    signal,
    gating,
    low_rank,
    dt_weight,
    dt_bias,
    decay_rate,
    skip_gain,
    coef_in,
    coef_out,
    segment_ids,
    out_grad,
):
    sig_f = signal[0].astype(jnp.float32)
    gate_f = gating[0].astype(jnp.float32)
    cot_f = out_grad[0].astype(jnp.float32)
    low_rows = low_rank[0]
    seg_row = segment_ids[0]
    tokens_here = sig_f.shape[0]
    num_blocks = tokens_here // step_block
    packed = jnp.concatenate([decay_rate, skip_gain[None, :], dt_bias[None, :]], 0)
    params_all = lax.all_gather(packed, "fsdp", axis=1, tiled=True)
    rate_all = params_all[:-2]
    skip_all = params_all[-2]
    bias_all = params_all[-1]
    dt_raw = (
        jnp.dot(
            low_rows,
            lax.all_gather(dt_weight, "fsdp", axis=1, tiled=True),
            preferred_element_type=jnp.float32,
        )
        + bias_all[None, :]
    )
    delta = jax.nn.softplus(dt_raw)
    before = from_behind(seg_row[-1:], "seq", 1)
    prev_seg = jnp.concatenate([before, seg_row[:-1]])
    keep = (seg_row == prev_seg).astype(jnp.float32)
    sig_gate = jax.nn.sigmoid(gate_f)
    out_adj = cot_f * gate_f * sig_gate

    def blocked(array):
        return array.reshape((num_blocks, step_block) + array.shape[1:])

    delta_b = blocked(delta)
    keep_b = blocked(keep)
    sig_b = blocked(sig_f)
    inc_b = blocked(coef_in[0].T)
    outc_b = blocked(coef_out[0].T)
    adj_b = blocked(out_adj)
    zeros_state = jnp.zeros(rate_all.shape, jnp.float32)

    def decay_of(d_row, k_val):
        return jnp.exp(-d_row[None, :] * rate_all) * k_val

    def forward_block(state, items):
        d_blk, k_blk, s_blk, b_blk = items
        start_state = state
        for offset in range(step_block):
            state = (
                decay_of(d_blk[offset], k_blk[offset]) * state
                + (d_blk[offset] * s_blk[offset])[None, :] * b_blk[offset][:, None]
            )
        return (state, start_state)

    local_end, local_starts = lax.scan(forward_block, zeros_state, (delta_b, keep_b, sig_b, inc_b))

    def adjoint_block(carried, items):
        d_blk, k_blk, c_blk, a_blk = items
        for offset in reversed(range(step_block)):
            adj = c_blk[offset][:, None] * a_blk[offset][None, :] + carried
            carried = decay_of(d_blk[offset], k_blk[offset]) * adj
        return (carried, None)

    local_back, _ = lax.scan(
        adjoint_block, zeros_state, (delta_b, keep_b, outc_b, adj_b), reverse=True
    )
    whole_decay = jnp.exp(-rate_all * jnp.sum(delta, 0)[None, :]) * jnp.prod(keep)
    hops = lax.axis_size("seq") - 1

    def forward_hop(turn, incoming):
        return from_behind(whole_decay * incoming + local_end, "seq", 1)

    def backward_hop(turn, incoming):
        return from_behind(whole_decay * incoming + local_back, "seq", -1)

    state_in = lax.fori_loop(0, hops, forward_hop, zeros_state)
    adjoint_in = lax.fori_loop(0, hops, backward_hop, zeros_state)
    block_sums = jnp.sum(delta_b, 1)
    before_sums = jnp.cumsum(block_sums, 0) - block_sums
    block_keep = jnp.prod(keep_b, 1)
    before_keep = jnp.concatenate([jnp.ones((1,), jnp.float32), jnp.cumprod(block_keep)[:-1]])
    true_starts = (
        local_starts
        + jnp.exp(-rate_all[None] * before_sums[:, None, :])
        * before_keep[:, None, None]
        * state_in[None]
    )

    def full_block(running, items):
        carried, rate_grad = running
        start_state, d_blk, k_blk, s_blk, b_blk, c_blk, a_blk = items
        decays = [decay_of(d_blk[offset], k_blk[offset]) for offset in range(step_block)]
        history = []
        state = start_state
        for offset in range(step_block):
            state = (
                decays[offset] * state
                + (d_blk[offset] * s_blk[offset])[None, :] * b_blk[offset][:, None]
            )
            history.append(state)
        scan_rows = [
            jnp.sum(c_blk[offset][:, None] * history[offset], 0) + skip_all * s_blk[offset]
            for offset in range(step_block)
        ]
        outc_rows = [
            jnp.sum(history[offset] * a_blk[offset][None, :], 1) for offset in range(step_block)
        ]
        inc_rows = [None] * step_block
        sig_rows = [None] * step_block
        delta_rows = [None] * step_block
        for offset in reversed(range(step_block)):
            prior = history[offset - 1] if offset > 0 else start_state
            adj = c_blk[offset][:, None] * a_blk[offset][None, :] + carried
            inc_rows[offset] = jnp.sum(adj * (d_blk[offset] * s_blk[offset])[None, :], 1)
            sig_rows[offset] = (
                d_blk[offset] * jnp.sum(adj * b_blk[offset][:, None], 0) + skip_all * a_blk[offset]
            )
            delta_rows[offset] = jnp.sum(
                adj
                * (
                    b_blk[offset][:, None] * s_blk[offset][None, :]
                    - rate_all * decays[offset] * prior
                ),
                0,
            )
            rate_grad = rate_grad - adj * prior * decays[offset] * d_blk[offset][None, :]
            carried = decays[offset] * adj
        return (
            (carried, rate_grad),
            (
                jnp.stack(scan_rows),
                jnp.stack(outc_rows),
                jnp.stack(inc_rows),
                jnp.stack(sig_rows),
                jnp.stack(delta_rows),
            ),
        )

    (_, rate_grad), results = lax.scan(
        full_block,
        (adjoint_in, zeros_state),
        (true_starts, delta_b, keep_b, sig_b, inc_b, outc_b, adj_b),
        reverse=True,
    )
    scan_out = results[0].reshape(tokens_here, -1)
    outc_grad = results[1].reshape(tokens_here, -1)
    inc_grad = results[2].reshape(tokens_here, -1)
    sig_grad = results[3].reshape(tokens_here, -1)
    delta_grad = results[4].reshape(tokens_here, -1)
    gate_grad = cot_f * scan_out * sig_gate * (1.0 + gate_f * (1.0 - sig_gate))
    raw_grad = delta_grad * jax.nn.sigmoid(dt_raw)
    raw_rounded = raw_grad.astype(jnp.bfloat16)
    portion = lax.all_gather(dt_weight, "fsdp", axis=1, tiled=True)
    columns = lax.slice_in_dim(raw_rounded, 0, portion.shape[1], axis=1)
    low_grad = jnp.zeros((tokens_here, low_rows.shape[1]), jnp.float32) + lax.dot_general(
        columns, portion, (((1,), (1,)), ((), ())), preferred_element_type=jnp.float32
    )
    small_part = jnp.concatenate(
        [rate_grad, jnp.sum(sig_f * out_adj, 0)[None, :], jnp.sum(raw_grad, 0)[None, :]], 0
    )
    weight_part = lax.dot_general(
        low_rows, raw_rounded, (((0,), (0,)), ((), ())), preferred_element_type=jnp.float32
    )
    weight_share, small_share = (
        lax.psum_scatter(weight_part, "fsdp", scatter_dimension=1, tiled=True),
        lax.psum_scatter(small_part, "fsdp", scatter_dimension=1, tiled=True),
    )
    weight_share, small_share = lax.psum((weight_share, small_share), "seq")
    return (
        sig_grad.astype(jnp.bfloat16)[None],
        gate_grad.astype(jnp.bfloat16)[None],
        low_grad[None],
        inc_grad.T[None],
        outc_grad.T[None],
        weight_share,
        small_share[:-2],
        small_share[-2],
        small_share[-1],
    )


def solution(mesh):
    return jax.shard_map(
        shards,
        mesh=mesh,
        in_specs=(
            P("fsdp", "seq", None),
            P("fsdp", "seq", None),
            P("fsdp", "seq", None),
            P(None, "fsdp"),
            P("fsdp"),
            P(None, "fsdp"),
            P("fsdp"),
            P("fsdp", None, "seq"),
            P("fsdp", None, "seq"),
            P("fsdp", "seq"),
            P("fsdp", "seq", None),
        ),
        out_specs=(
            P("fsdp", "seq", None),
            P("fsdp", "seq", None),
            P("fsdp", "seq", None),
            P("fsdp", None, "seq"),
            P("fsdp", None, "seq"),
            P(None, "fsdp"),
            P(None, "fsdp"),
            P("fsdp"),
            P("fsdp"),
        ),
        check_vma=False,
    )
```

profile of v0, /device:TPU:4, one launch (start us, length us, event | category | flops | bytes accessed | tf_op | source)
XLA Modules:
  0.0 1848.8 jit_solution(709207774440535963)
XLA Ops:
  21.7 21.6 %all_gather.7 = f32[18,8192]{1,0:T(8,128)S(1)} all-gather(f32[18,512]{1,0:T(8,128)S(1)} %pad_maximum_fusion.1), channel_id=1, replica_groups=mesh['seq'=8,'fsdp'=16] {'fsdp'}, dimensions={1}, use_global_device_ids=true | all-gather | bytes 626688 | tf_op jit(solution)/shard_map/all_gather | solution.py:36
  43.3 7.4 multiply_reduce_fusion.79
  54.6 12.9 all-gather.2.cloned.1.call-done
  67.5 10.3 compare_select_fusion
  79.3 158.9 %while.77 = (s32[]{:T(128)}, f32[16,8192]{1,0:T(8,128)S(1)}, f32[8,16,8192]{2,1,0:T(8,128)}, f32[16,8192]{1,0:T(8,128)S(1)}, f32[8,16]{1,0:T(8,128)}, /*index=5*...) while((s32[]{:T(128)}, f32[16,8192]{1,0:T(8,128)S(1)}, ...), condition=%wide.region_3.4_spmd.clone, body=%wide.region_2.3_spmd.clone.sunk | while | flops 10747923 | bytes 4722547 | solution.py:88
  87.2 12.1 add_multiply_fusion.2
  107.2 12.1 add_multiply_fusion.2
  126.9 12.1 add_multiply_fusion.2
  146.5 12.1 add_multiply_fusion.2
  166.4 12.1 add_multiply_fusion.2
  186.5 12.1 add_multiply_fusion.2
  206.3 12.1 add_multiply_fusion.2
  226.1 12.1 add_multiply_fusion.2
  240.5 163.9 %while.78 = (s32[]{:T(128)}, f32[16,8192]{1,0:T(8,128)S(1)}, f32[8,16,8192]{2,1,0:T(8,128)}, f32[8,16,8192]{2,1,0:T(8,128)}, f32[16,8192]{1,0:T(8,128)S(1)}, /*i...) while((s32[]{:T(128)}, f32[16,8192]{1,0:T(8,128)S(1)}, ...), condition=%wide.region_7.8_spmd.clone, body=%wide.region_6.7_spmd.clone.sunk | while | flops 11010066 | bytes 5771116 | solution.py:79
  248.8 12.1 multiply_add_fusion.55
  269.4 12.1 multiply_add_fusion.55
  289.9 12.1 multiply_add_fusion.55
  310.3 12.1 multiply_add_fusion.55
  330.7 12.1 multiply_add_fusion.55
  351.3 12.1 multiply_add_fusion.55
  372.0 12.1 multiply_add_fusion.55
  392.4 12.1 multiply_add_fusion.55
  410.4 102.2 %while.76 = (s32[]{:T(128)}, f32[16,8192]{1,0:T(8,128)S(1)}, f32[16,8192]{1,0:T(8,128)S(1)}, f32[16,8192]{1,0:T(8,128)S(1)}, s32[]{:T(128)}) while((s32[]{:T(128)}, f32[16,8192]{1,0:T(8,128)S(1)}, f32[16,8192]{1,0:T(8,128)S(1)}, f32[16,8192]{1,0:T(8,128)S(1)}, s32[]{:T(128)}) %tuple.585), condition=%wide.region_13.14_spmd, body=%wide.region_12.13_spmd.sunk | while | flops 262146 | bytes 4194405 | solution.py:100
  414.0 11.5 collective-permute-done.1
  430.1 10.7 collective-permute-done.1
  445.3 9.8 collective-permute-done.1
  459.6 8.9 collective-permute-done.1
  474.7 8.0 collective-permute-done.1
  482.8 8.0 collective-permute-start.1
  490.8 7.0 collective-permute-done.1
  497.9 8.0 collective-permute-start.1
  506.0 6.6 collective-permute-done.1
  517.8 115.7 %while.75 = (s32[]{:T(128)}, f32[16,8192]{1,0:T(8,128)S(1)}, f32[16,8192]{1,0:T(8,128)S(1)}, f32[16,8192]{1,0:T(8,128)S(1)}, s32[]{:T(128)}) while((s32[]{:T(128)}, f32[16,8192]{1,0:T(8,128)S(1)}, f32[16,8192]{1,0:T(8,128)S(1)}, f32[16,8192]{1,0:T(8,128)S(1)}, s32[]{:T(128)}) %tuple.601), condition=%wide.region_5.6_spmd, body=%wide.region_4.5_spmd.sunk | while | flops 262146 | bytes 4194405 | solution.py:101
  519.2 13.9 collective-permute-done
  534.5 13.9 collective-permute-done
  549.7 13.9 collective-permute-done
  564.9 16.0 collective-permute-done
  582.3 16.4 collective-permute-done
  600.1 17.8 collective-permute-done
  619.3 14.2 collective-permute-done
  639.6 924.6 %while.79 = (s32[]{:T(128)}, f32[16,8192]{1,0:T(8,128)S(1)}, f32[16,8192]{1,0:T(8,128)}, f32[8,16,8192]{2,1,0:T(8,128)}, f32[8,16,16]{2,1,0:T(8,128)}, /*index=5...) while((s32[]{:T(128)}, f32[16,8192]{1,0:T(8,128)S(1)}, ...), condition=%wide.region_95.96_spmd.clone, body=%wide.region_14.95_spmd.clone.sunk | while | flops 74710544 | bytes 95165264 | solution.py:163
  684.4 17.7 multiply_reduce_fusion.89
  702.6 17.1 fusion.239
  798.1 17.7 multiply_reduce_fusion.89
  816.3 17.2 fusion.239
  912.6 17.7 multiply_reduce_fusion.89
  930.8 17.2 fusion.239
  1026.2 17.7 multiply_reduce_fusion.89
  1044.4 17.2 fusion.239
  1140.0 17.7 multiply_reduce_fusion.89
  1158.2 17.2 fusion.239
  1253.2 17.7 multiply_reduce_fusion.89
  1271.4 17.2 fusion.239
  1367.0 17.7 multiply_reduce_fusion.89
  1385.2 17.2 fusion.239
  1480.2 17.7 multiply_reduce_fusion.89
  1498.4 17.2 fusion.239
  1568.8 8.1 convolution_bitcast_fusion
  1579.0 105.3 %reduce-scatter.3.cloned.1.call-done = f32[512,512]{0,1:T(8,128)} async-done(((f32[512,8192]{0,1:T(8,128)}), f32[512,512]{0,1:T(8,128)}) %reduce-scatter.3.cloned.1.call-update) | async-done | bytes 1048592 | tf_op jit(solution)/shard_map/reduce_scatter | solution.py:189
  1684.4 6.5 fusion.144
  1692.2 7.0 convolution_bitcast_fusion.1
  1699.2 43.9 %reduce-scatter.5.cloned.1.call-done = f32[18,512]{1,0:T(8,128)} async-done(((f32[18,8192]{1,0:T(8,128)}), f32[18,512]{1,0:T(8,128)}) %reduce-scatter.5.cloned.1.call-update) | async-done | bytes 36880 | tf_op jit(solution)/shard_map/reduce_scatter | solution.py:190
  1743.1 43.1 %psum.15 = f32[18,512]{1,0:T(8,128)S(1)} all-reduce(f32[18,512]{1,0:T(8,128)} %reduce-scatter.5.cloned.1.call-done), channel_id=1, replica_groups=mesh['seq'=8,'fsdp'=16] {'seq'}, use_global_device_ids=true, to_apply=%region_101.102 | all-reduce | flops 9216 | bytes 73728 | tf_op jit(solution)/shard_map/psum | solution.py:192
  1787.5 51.9 %all-reduce.2.cloned.1.call-done = f32[512,512]{0,1:T(8,128)} async-done(((f32[512,512]{0,1:T(8,128)}), f32[512,512]{0,1:T(8,128)}) %all-reduce.2.cloned.1.call-update) | async-done | bytes 1048592 | tf_op jit(solution)/shard_map/psum | solution.py:192
  (2643 shorter events, 830.2 us)
Async XLA Ops:
  7.2 60.3 %copy-start = (bf16[1,128,512]{2,1,0:T(8,128)(2,1)S(1)}, bf16[1,128,512]{2,1,0:T(8,128)(2,1)}, u32[]{:S(2)}) copy-start(bf16[1,128,512]{2,1,0:T(8,128)(2,1)} %param.23) | copy-start | bytes 393220
  7.2 60.2 %all-gather.2.cloned.1.call-start = ((), (), s32[]{:S(2)}) async-start(), calls=%async_computation.2 | async-start | bytes 8912896 | tf_op jit(solution)/shard_map/all_gather | solution.py:43
  8.0 1676.3 %reduce-scatter.3.cloned.1.call-start = ((), (), s32[]{:S(2)}) async-start(), calls=%async_computation.3 | async-start | bytes 17825792 | tf_op jit(solution)/shard_map/reduce_scatter | solution.py:189
  9.3 43.0 %collective-permute-start.2 = (s32[1]{0:T(128)}, s32[1]{0:T(128)}, u32[]{:S(2)}, u32[]{:S(2)}) collective-permute-start(s32[1]{0:T(128)} %bitcast.5), channel_id=1, source_target_pairs={{0,16},{16,32},{32,48},{48,64},{64,80},{80,96},{96,112},{1,17},{17... | collective-permute-start | bytes 20 | tf_op jit(solution)/shard_map/ppermute | solution.py:12
  410.5 15.1 collective-permute-start.1
  425.6 15.2 collective-permute-start.1
  440.9 14.2 collective-permute-start.1
  455.2 13.3 collective-permute-start.1
  468.6 14.1 collective-permute-start.1
  482.8 15.1 collective-permute-start.1
  497.9 14.7 collective-permute-start.1
  517.9 15.2 collective-permute-start
  533.2 15.2 collective-permute-start
  548.4 15.2 collective-permute-start
  563.6 17.3 collective-permute-start
  581.0 17.7 collective-permute-start
  598.8 19.1 %collective-permute-start = (f32[16,8192]{1,0:T(8,128)S(1)}, f32[16,8192]{1,0:T(8,128)S(1)}, u32[]{:S(2)}, u32[]{:S(2)}) collective-permute-start(f32[16,8192]{1,0:T(8,128)S(1)} %multiply_add_fusion.53), channel_id=1, source_target_pairs={{16,0},{32,16},{48,32},{64,48},{80,64},{96,80},{112,96},{17,1},{33... | collective-permute-start | bytes 1572872 | tf_op jit(solution)/shard_map/while/body/eval_jaxpr/ppermute | solution.py:12
  618.0 15.5 collective-permute-start
  664.2 38.0 %copy-start.56 = (f32[1,1,8192]{2,1,0:T(1,128)}, f32[1,1,8192]{2,1,0:T(1,128)S(1)}, u32[]{:S(2)}) copy-start(f32[1,1,8192]{2,1,0:T(1,128)S(1)} %get-tuple-element.2088) | copy-start | bytes 98308 | tf_op jit(solution)/shard_map/while
  664.2 38.0 %copy-start.59 = (f32[1,1,8192]{2,1,0:T(1,128)}, f32[1,1,8192]{2,1,0:T(1,128)S(1)}, u32[]{:S(2)}) copy-start(f32[1,1,8192]{2,1,0:T(1,128)S(1)} %get-tuple-element.2084) | copy-start | bytes 98308 | tf_op jit(solution)/shard_map/while
  664.2 38.0 %copy-start.62 = (f32[1,1,8192]{2,1,0:T(1,128)}, f32[1,1,8192]{2,1,0:T(1,128)S(1)}, u32[]{:S(2)}) copy-start(f32[1,1,8192]{2,1,0:T(1,128)S(1)} %get-tuple-element.1965) | copy-start | bytes 98308 | tf_op jit(solution)/shard_map/while
  664.2 38.0 %copy-start.64 = (f32[1,1,8192]{2,1,0:T(1,128)}, f32[1,1,8192]{2,1,0:T(1,128)S(1)}, u32[]{:S(2)}) copy-start(f32[1,1,8192]{2,1,0:T(1,128)S(1)} %get-tuple-element.2080) | copy-start | bytes 98308 | tf_op jit(solution)/shard_map/while
  664.2 38.0 %copy-start.67 = (f32[1,1,8192]{2,1,0:T(1,128)}, f32[1,1,8192]{2,1,0:T(1,128)S(1)}, u32[]{:S(2)}) copy-start(f32[1,1,8192]{2,1,0:T(1,128)S(1)} %get-tuple-element.2076) | copy-start | bytes 98308 | tf_op jit(solution)/shard_map/while
  664.2 38.0 %copy-start.70 = (f32[1,1,8192]{2,1,0:T(1,128)}, f32[1,1,8192]{2,1,0:T(1,128)S(1)}, u32[]{:S(2)}) copy-start(f32[1,1,8192]{2,1,0:T(1,128)S(1)} %get-tuple-element.2072) | copy-start | bytes 98308 | tf_op jit(solution)/shard_map/while
  664.2 38.0 %copy-start.73 = (f32[1,1,8192]{2,1,0:T(1,128)}, f32[1,1,8192]{2,1,0:T(1,128)S(1)}, u32[]{:S(2)}) copy-start(f32[1,1,8192]{2,1,0:T(1,128)S(1)} %get-tuple-element.2068) | copy-start | bytes 98308 | tf_op jit(solution)/shard_map/while
  664.2 38.0 %copy-start.76 = (f32[1,1,8192]{2,1,0:T(1,128)}, f32[1,1,8192]{2,1,0:T(1,128)S(1)}, u32[]{:S(2)}) copy-start(f32[1,1,8192]{2,1,0:T(1,128)S(1)} %get-tuple-element.2064) | copy-start | bytes 98308 | tf_op jit(solution)/shard_map/while
  777.5 38.4 %copy-start.56 = (f32[1,1,8192]{2,1,0:T(1,128)}, f32[1,1,8192]{2,1,0:T(1,128)S(1)}, u32[]{:S(2)}) copy-start(f32[1,1,8192]{2,1,0:T(1,128)S(1)} %get-tuple-element.2088) | copy-start | bytes 98308 | tf_op jit(solution)/shard_map/while
  777.5 38.4 %copy-start.59 = (f32[1,1,8192]{2,1,0:T(1,128)}, f32[1,1,8192]{2,1,0:T(1,128)S(1)}, u32[]{:S(2)}) copy-start(f32[1,1,8192]{2,1,0:T(1,128)S(1)} %get-tuple-element.2084) | copy-start | bytes 98308 | tf_op jit(solution)/shard_map/while
  777.5 38.4 %copy-start.62 = (f32[1,1,8192]{2,1,0:T(1,128)}, f32[1,1,8192]{2,1,0:T(1,128)S(1)}, u32[]{:S(2)}) copy-start(f32[1,1,8192]{2,1,0:T(1,128)S(1)} %get-tuple-element.1965) | copy-start | bytes 98308 | tf_op jit(solution)/shard_map/while
  777.5 38.4 %copy-start.64 = (f32[1,1,8192]{2,1,0:T(1,128)}, f32[1,1,8192]{2,1,0:T(1,128)S(1)}, u32[]{:S(2)}) copy-start(f32[1,1,8192]{2,1,0:T(1,128)S(1)} %get-tuple-element.2080) | copy-start | bytes 98308 | tf_op jit(solution)/shard_map/while
  777.5 38.3 %copy-start.67 = (f32[1,1,8192]{2,1,0:T(1,128)}, f32[1,1,8192]{2,1,0:T(1,128)S(1)}, u32[]{:S(2)}) copy-start(f32[1,1,8192]{2,1,0:T(1,128)S(1)} %get-tuple-element.2076) | copy-start | bytes 98308 | tf_op jit(solution)/shard_map/while
  777.5 38.3 %copy-start.70 = (f32[1,1,8192]{2,1,0:T(1,128)}, f32[1,1,8192]{2,1,0:T(1,128)S(1)}, u32[]{:S(2)}) copy-start(f32[1,1,8192]{2,1,0:T(1,128)S(1)} %get-tuple-element.2072) | copy-start | bytes 98308 | tf_op jit(solution)/shard_map/while
  777.6 38.3 %copy-start.73 = (f32[1,1,8192]{2,1,0:T(1,128)}, f32[1,1,8192]{2,1,0:T(1,128)S(1)}, u32[]{:S(2)}) copy-start(f32[1,1,8192]{2,1,0:T(1,128)S(1)} %get-tuple-element.2068) | copy-start | bytes 98308 | tf_op jit(solution)/shard_map/while
  777.6 38.3 %copy-start.76 = (f32[1,1,8192]{2,1,0:T(1,128)}, f32[1,1,8192]{2,1,0:T(1,128)S(1)}, u32[]{:S(2)}) copy-start(f32[1,1,8192]{2,1,0:T(1,128)S(1)} %get-tuple-element.2064) | copy-start | bytes 98308 | tf_op jit(solution)/shard_map/while
  892.2 38.2 %copy-start.56 = (f32[1,1,8192]{2,1,0:T(1,128)}, f32[1,1,8192]{2,1,0:T(1,128)S(1)}, u32[]{:S(2)}) copy-start(f32[1,1,8192]{2,1,0:T(1,128)S(1)} %get-tuple-element.2088) | copy-start | bytes 98308 | tf_op jit(solution)/shard_map/while
  892.2 38.2 %copy-start.59 = (f32[1,1,8192]{2,1,0:T(1,128)}, f32[1,1,8192]{2,1,0:T(1,128)S(1)}, u32[]{:S(2)}) copy-start(f32[1,1,8192]{2,1,0:T(1,128)S(1)} %get-tuple-element.2084) | copy-start | bytes 98308 | tf_op jit(solution)/shard_map/while
  892.2 38.2 %copy-start.62 = (f32[1,1,8192]{2,1,0:T(1,128)}, f32[1,1,8192]{2,1,0:T(1,128)S(1)}, u32[]{:S(2)}) copy-start(f32[1,1,8192]{2,1,0:T(1,128)S(1)} %get-tuple-element.1965) | copy-start | bytes 98308 | tf_op jit(solution)/shard_map/while
  892.2 38.2 %copy-start.64 = (f32[1,1,8192]{2,1,0:T(1,128)}, f32[1,1,8192]{2,1,0:T(1,128)S(1)}, u32[]{:S(2)}) copy-start(f32[1,1,8192]{2,1,0:T(1,128)S(1)} %get-tuple-element.2080) | copy-start | bytes 98308 | tf_op jit(solution)/shard_map/while
  892.2 38.2 %copy-start.67 = (f32[1,1,8192]{2,1,0:T(1,128)}, f32[1,1,8192]{2,1,0:T(1,128)S(1)}, u32[]{:S(2)}) copy-start(f32[1,1,8192]{2,1,0:T(1,128)S(1)} %get-tuple-element.2076) | copy-start | bytes 98308 | tf_op jit(solution)/shard_map/while
  892.2 38.2 %copy-start.70 = (f32[1,1,8192]{2,1,0:T(1,128)}, f32[1,1,8192]{2,1,0:T(1,128)S(1)}, u32[]{:S(2)}) copy-start(f32[1,1,8192]{2,1,0:T(1,128)S(1)} %get-tuple-element.2072) | copy-start | bytes 98308 | tf_op jit(solution)/shard_map/while
  892.2 38.2 %copy-start.73 = (f32[1,1,8192]{2,1,0:T(1,128)}, f32[1,1,8192]{2,1,0:T(1,128)S(1)}, u32[]{:S(2)}) copy-start(f32[1,1,8192]{2,1,0:T(1,128)S(1)} %get-tuple-element.2068) | copy-start | bytes 98308 | tf_op jit(solution)/shard_map/while
  892.2 38.2 %copy-start.76 = (f32[1,1,8192]{2,1,0:T(1,128)}, f32[1,1,8192]{2,1,0:T(1,128)S(1)}, u32[]{:S(2)}) copy-start(f32[1,1,8192]{2,1,0:T(1,128)S(1)} %get-tuple-element.2064) | copy-start | bytes 98308 | tf_op jit(solution)/shard_map/while
  1119.7 38.0 %copy-start.56 = (f32[1,1,8192]{2,1,0:T(1,128)}, f32[1,1,8192]{2,1,0:T(1,128)S(1)}, u32[]{:S(2)}) copy-start(f32[1,1,8192]{2,1,0:T(1,128)S(1)} %get-tuple-element.2088) | copy-start | bytes 98308 | tf_op jit(solution)/shard_map/while
  1119.7 38.0 %copy-start.59 = (f32[1,1,8192]{2,1,0:T(1,128)}, f32[1,1,8192]{2,1,0:T(1,128)S(1)}, u32[]{:S(2)}) copy-start(f32[1,1,8192]{2,1,0:T(1,128)S(1)} %get-tuple-element.2084) | copy-start | bytes 98308 | tf_op jit(solution)/shard_map/while
  1119.8 38.0 %copy-start.62 = (f32[1,1,8192]{2,1,0:T(1,128)}, f32[1,1,8192]{2,1,0:T(1,128)S(1)}, u32[]{:S(2)}) copy-start(f32[1,1,8192]{2,1,0:T(1,128)S(1)} %get-tuple-element.1965) | copy-start | bytes 98308 | tf_op jit(solution)/shard_map/while
  1119.8 38.0 %copy-start.64 = (f32[1,1,8192]{2,1,0:T(1,128)}, f32[1,1,8192]{2,1,0:T(1,128)S(1)}, u32[]{:S(2)}) copy-start(f32[1,1,8192]{2,1,0:T(1,128)S(1)} %get-tuple-element.2080) | copy-start | bytes 98308 | tf_op jit(solution)/shard_map/while
  1232.9 38.1 %copy-start.56 = (f32[1,1,8192]{2,1,0:T(1,128)}, f32[1,1,8192]{2,1,0:T(1,128)S(1)}, u32[]{:S(2)}) copy-start(f32[1,1,8192]{2,1,0:T(1,128)S(1)} %get-tuple-element.2088) | copy-start | bytes 98308 | tf_op jit(solution)/shard_map/while
  1232.9 38.1 %copy-start.59 = (f32[1,1,8192]{2,1,0:T(1,128)}, f32[1,1,8192]{2,1,0:T(1,128)S(1)}, u32[]{:S(2)}) copy-start(f32[1,1,8192]{2,1,0:T(1,128)S(1)} %get-tuple-element.2084) | copy-start | bytes 98308 | tf_op jit(solution)/shard_map/while
  1232.9 38.1 %copy-start.62 = (f32[1,1,8192]{2,1,0:T(1,128)}, f32[1,1,8192]{2,1,0:T(1,128)S(1)}, u32[]{:S(2)}) copy-start(f32[1,1,8192]{2,1,0:T(1,128)S(1)} %get-tuple-element.1965) | copy-start | bytes 98308 | tf_op jit(solution)/shard_map/while
  1232.9 38.1 %copy-start.64 = (f32[1,1,8192]{2,1,0:T(1,128)}, f32[1,1,8192]{2,1,0:T(1,128)S(1)}, u32[]{:S(2)}) copy-start(f32[1,1,8192]{2,1,0:T(1,128)S(1)} %get-tuple-element.2080) | copy-start | bytes 98308 | tf_op jit(solution)/shard_map/while
  1232.9 38.1 %copy-start.67 = (f32[1,1,8192]{2,1,0:T(1,128)}, f32[1,1,8192]{2,1,0:T(1,128)S(1)}, u32[]{:S(2)}) copy-start(f32[1,1,8192]{2,1,0:T(1,128)S(1)} %get-tuple-element.2076) | copy-start | bytes 98308 | tf_op jit(solution)/shard_map/while
  1232.9 38.1 %copy-start.70 = (f32[1,1,8192]{2,1,0:T(1,128)}, f32[1,1,8192]{2,1,0:T(1,128)S(1)}, u32[]{:S(2)}) copy-start(f32[1,1,8192]{2,1,0:T(1,128)S(1)} %get-tuple-element.2072) | copy-start | bytes 98308 | tf_op jit(solution)/shard_map/while
  1232.9 38.1 %copy-start.73 = (f32[1,1,8192]{2,1,0:T(1,128)}, f32[1,1,8192]{2,1,0:T(1,128)S(1)}, u32[]{:S(2)}) copy-start(f32[1,1,8192]{2,1,0:T(1,128)S(1)} %get-tuple-element.2068) | copy-start | bytes 98308 | tf_op jit(solution)/shard_map/while
  1232.9 38.1 %copy-start.76 = (f32[1,1,8192]{2,1,0:T(1,128)}, f32[1,1,8192]{2,1,0:T(1,128)S(1)}, u32[]{:S(2)}) copy-start(f32[1,1,8192]{2,1,0:T(1,128)S(1)} %get-tuple-element.2064) | copy-start | bytes 98308 | tf_op jit(solution)/shard_map/while
  1346.6 38.2 %copy-start.56 = (f32[1,1,8192]{2,1,0:T(1,128)}, f32[1,1,8192]{2,1,0:T(1,128)S(1)}, u32[]{:S(2)}) copy-start(f32[1,1,8192]{2,1,0:T(1,128)S(1)} %get-tuple-element.2088) | copy-start | bytes 98308 | tf_op jit(solution)/shard_map/while
  1346.6 38.2 %copy-start.59 = (f32[1,1,8192]{2,1,0:T(1,128)}, f32[1,1,8192]{2,1,0:T(1,128)S(1)}, u32[]{:S(2)}) copy-start(f32[1,1,8192]{2,1,0:T(1,128)S(1)} %get-tuple-element.2084) | copy-start | bytes 98308 | tf_op jit(solution)/shard_map/while
  1346.6 38.1 %copy-start.62 = (f32[1,1,8192]{2,1,0:T(1,128)}, f32[1,1,8192]{2,1,0:T(1,128)S(1)}, u32[]{:S(2)}) copy-start(f32[1,1,8192]{2,1,0:T(1,128)S(1)} %get-tuple-element.1965) | copy-start | bytes 98308 | tf_op jit(solution)/shard_map/while
  1346.6 38.1 %copy-start.64 = (f32[1,1,8192]{2,1,0:T(1,128)}, f32[1,1,8192]{2,1,0:T(1,128)S(1)}, u32[]{:S(2)}) copy-start(f32[1,1,8192]{2,1,0:T(1,128)S(1)} %get-tuple-element.2080) | copy-start | bytes 98308 | tf_op jit(solution)/shard_map/while
  1346.6 38.1 %copy-start.67 = (f32[1,1,8192]{2,1,0:T(1,128)}, f32[1,1,8192]{2,1,0:T(1,128)S(1)}, u32[]{:S(2)}) copy-start(f32[1,1,8192]{2,1,0:T(1,128)S(1)} %get-tuple-element.2076) | copy-start | bytes 98308 | tf_op jit(solution)/shard_map/while
  1346.6 38.1 %copy-start.70 = (f32[1,1,8192]{2,1,0:T(1,128)}, f32[1,1,8192]{2,1,0:T(1,128)S(1)}, u32[]{:S(2)}) copy-start(f32[1,1,8192]{2,1,0:T(1,128)S(1)} %get-tuple-element.2072) | copy-start | bytes 98308 | tf_op jit(solution)/shard_map/while
  1346.6 38.1 %copy-start.73 = (f32[1,1,8192]{2,1,0:T(1,128)}, f32[1,1,8192]{2,1,0:T(1,128)S(1)}, u32[]{:S(2)}) copy-start(f32[1,1,8192]{2,1,0:T(1,128)S(1)} %get-tuple-element.2068) | copy-start | bytes 98308 | tf_op jit(solution)/shard_map/while
  1346.6 38.1 %copy-start.76 = (f32[1,1,8192]{2,1,0:T(1,128)}, f32[1,1,8192]{2,1,0:T(1,128)S(1)}, u32[]{:S(2)}) copy-start(f32[1,1,8192]{2,1,0:T(1,128)S(1)} %get-tuple-element.2064) | copy-start | bytes 98308 | tf_op jit(solution)/shard_map/while
  1576.9 166.2 %reduce-scatter.5.cloned.1.call-start = ((), (), s32[]{:S(2)}) async-start(), calls=%async_computation.5 | async-start | bytes 835584 | tf_op jit(solution)/shard_map/reduce_scatter | solution.py:190
  1578.9 260.4 %all-reduce.2.cloned.1.call-start = ((), (), s32[]{:S(2)}) async-start(), calls=%async_computation.4 | async-start | bytes 2097152 | tf_op jit(solution)/shard_map/psum | solution.py:192
  (1023 other events, 17452.5 us)
Sparse Core Ops, SparseCore 0:
  9.7 57.7 all-gather.1
  1577.1 107.2 reduce-scatter.2
  1687.2 55.8 reduce-scatter.4
  1745.6 93.6 all-reduce.1
where the time goes:
time: 1880 us; the launch traced here: 1850 us
  other arithmetic  994 us (53%)
  waiting for transfers between devices  383 us (20%)
  local copies, waits for them, and re-layouts  286 us (15%)
  blocking collectives  64.7 us (3%)
  starting transfers between devices  52.5 us (3%)
  loops' own time  28.8 us (2%)
  matrix products  25.3 us (1%)
    reduce_sum x64, other arithmetic, full_block(): jnp.sum(adj * (b_blk[offset][:, None] * s_blk[offset][None, :] - rate_all...  360 us
    ppermute x15, waiting for transfers between devices, from_behind(): return lax.ppermute(x, axis, pairs)  169 us
    sub x8, other arithmetic, full_block(): rate_grad - adj * prior * decays[offset] * d_blk[offset][None, :]  137 us
    neg x120, other arithmetic, decay_of(): return jnp.exp(-d_row[None, :] * rate_all) * k_val  126 us
    reduce_scatter x1, waiting for transfers between devices, shards(): lax.psum_scatter(weight_part, 'fsdp', scatter_dimension=1, tiled=True)  105 us
    add x8, other arithmetic, forward_block(): decay_of(d_blk[offset], k_blk[offset]) * state  96.7 us
    mul x8, other arithmetic, adjoint_block(): carried = decay_of(d_blk[offset], k_blk[offset]) * adj  96.7 us
    ppermute x15, starting transfers between devices, from_behind(): return lax.ppermute(x, axis, pairs)  52.3 us
  transfers between devices with their start and end apart: 19, of which 18 were waited for; matrix products, arithmetic and copies ran while one was open for 2% of the time, Pallas kernels for 0%

commit v1 on v0

v1 whole, which is shorter than its diff:
```python
import functools, math
import jax, jax.numpy as jnp
from jax import lax
from jax.experimental import pallas as pl
from jax.experimental.pallas import tpu as pltpu
from jax.sharding import PartitionSpec as P

F32, BF16 = jnp.float32, jnp.bfloat16
LANES = 128
SUB = 16
LOG2E = math.log2(math.e)

def lanes(g):
    return slice(g * LANES, (g + 1) * LANES)

def prepare(low, w, bias, sig, gate, cot, keep):
    raw = jnp.dot(low, w, preferred_element_type=F32) + bias
    delta = jnp.maximum(raw, 0.0) + jnp.log1p(jnp.exp(-jnp.abs(raw)))
    s = sig.astype(F32)
    g = gate.astype(F32)
    sg = jax.nn.sigmoid(g)
    a = cot.astype(F32) * g * sg
    ks = jnp.concatenate([keep] * (raw.shape[1] // LANES), 1)
    dk = jnp.where(ks > 0, delta, jnp.inf)
    return raw, delta, dk, delta * s, a

def local_kernel(low, w, bias, rate, sig, gate, cot, keep, inb, outb, end, back, total, dk_s, ds_s, a_s):
    tokens, width = sig.shape
    groups = width // LANES
    raw, delta, dk, ds, a = prepare(low[...], w[...], bias[...], sig[...], gate[...], cot[...], keep[...])
    dk_s[...] = dk
    ds_s[...] = ds
    a_s[...] = a
    total[...] = jnp.sum(dk, 0, keepdims=True)
    states = rate.shape[0]
    nrate = [rate[:, lanes(g)] * (-LOG2E) for g in range(groups)]
    def body(i, carry):
        st, ad = list(carry[0]), list(carry[1])
        fb = pl.ds(pl.multiple_of(i * SUB, SUB), SUB)
        rb = pl.ds(pl.multiple_of(tokens - SUB - i * SUB, SUB), SUB)
        for u in range(SUB):
            t = i * SUB + u
            v = tokens - 1 - t
            bb = inb[pl.ds(pl.multiple_of(t * states, states), states), :]
            cc = outb[pl.ds(pl.multiple_of(v * states, states), states), :]
            for g in range(groups):
                dec = jnp.exp2(nrate[g] * dk_s.at[fb, lanes(g)][u:u + 1, :])
                st[g] = dec * st[g] + bb * ds_s.at[fb, lanes(g)][u:u + 1, :]
                dec2 = jnp.exp2(nrate[g] * dk_s.at[rb, lanes(g)][SUB - 1 - u:SUB - u, :])
                ad[g] = dec2 * (cc * a_s.at[rb, lanes(g)][SUB - 1 - u:SUB - u, :] + ad[g])
        return tuple(st), tuple(ad)
    z = tuple(jnp.zeros((states, LANES), F32) for _ in range(groups))
    st, ad = lax.fori_loop(0, tokens // SUB, body, (z, z))
    for g in range(groups):
        end[:, lanes(g)] = st[g]
        back[:, lanes(g)] = ad[g]

def full_kernel(low, w, bias, rate, skip, sig, gate, cot, keep, inb, outb, cmat, bmat, omat, s_in, a_in,
                g_sig, g_gate, g_low, g_inc, g_outc, dw, g_rate, g_skip, g_bias,
                dk_s, d_s, ds_s, a_s, r_s, hist, dec_s, hb0, hb1, ab0, ab1, al0, al1, zr0, zr1,
                ascan, ab16, db16, q_s, zz_s, oc_s, ic_s, *, lo):
    step = pl.program_id(0)
    tokens, width = sig.shape
    groups = width // LANES
    states = rate.shape[0]
    blk = SUB * states
    nblk = tokens // SUB
    raw, delta, dk, ds, a = prepare(low[...], w[...], bias[...], sig[...], gate[...], cot[...], keep[...])
    dk_s[...] = dk
    d_s[...] = delta
    ds_s[...] = ds
    a_s[...] = a
    r_s[...] = jax.nn.sigmoid(raw)

    def split(ref, x):
        hi = x.astype(BF16)
        lowp = (x - hi.astype(F32)).astype(BF16)
        for k in range(nblk):
            ref[2 * SUB * (k + 1):2 * SUB * (k + 1) + SUB, :] = hi[k * SUB:(k + 1) * SUB]
            ref[2 * SUB * (k + 1) + SUB:2 * SUB * (k + 2), :] = lowp[k * SUB:(k + 1) * SUB]
    split(ab16, a)
    split(db16, ds)

    @pl.when(step == 0)
    def _():
        oc_s[...] = jnp.zeros_like(oc_s)
        ic_s[...] = jnp.zeros_like(ic_s)
        g_low[...] = jnp.zeros_like(g_low)

    nrate = [rate[:, lanes(g)] * (-LOG2E) for g in range(groups)]
    st0 = tuple(s_in[:, lanes(g)] for g in range(groups))
    for g in range(groups):
        hist[0:states, lanes(g)] = st0[g]

    def nt(x, y):
        return lax.dot_general(x, y, (((1,), (1,)), ((), ())), preferred_element_type=F32)

    def fwd_vec(k, st, hb):
        fb = pl.ds(pl.multiple_of(k * SUB, SUB), SUB)
        for u in range(SUB):
            t = k * SUB + u
            row = pl.multiple_of(t * states, states)
            bb = inb[pl.ds(row, states), :]
            for g in range(groups):
                dec = jnp.exp2(nrate[g] * dk_s.at[fb, lanes(g)][u:u + 1, :])
                dec_s[pl.ds(row, states), lanes(g)] = dec
                st[g] = dec * st[g] + bb * ds_s.at[fb, lanes(g)][u:u + 1, :]
                hist[pl.ds(row + states, states), lanes(g)] = st[g]
                hb[u * states:(u + 1) * states, lanes(g)] = st[g].astype(BF16)
        return st

    def fwd_mat(k, hb):
        r32 = pl.multiple_of((k + 1) * 2 * SUB, 2 * SUB)
        r16 = pl.multiple_of((k + 1) * SUB, SUB)
        h = hb[...]
        y = jnp.dot(cmat[pl.ds(r32, 2 * SUB), :], h, preferred_element_type=F32)
        ascan[pl.ds(r16, SUB), :] = y[:SUB] + y[SUB:]
        o = nt(ab16[pl.ds(r32, 2 * SUB), :], h)
        oc_s[pl.ds(r16, SUB), :] += o[:SUB] + o[SUB:]

    def fwd(i, carry):
        st = fwd_vec(2 * i, list(carry), hb0)
        fwd_mat(2 * i - 1, hb1)
        st = fwd_vec(2 * i + 1, st, hb1)
        fwd_mat(2 * i, hb0)
        return tuple(st)
    lax.fori_loop(0, nblk // 2, fwd, st0)
    fwd_mat(nblk - 1, hb1)

    def bwd_vec(k, ca, rg, ab, al, zr):
        fb = pl.ds(pl.multiple_of(k * SUB, SUB), SUB)
        for u in reversed(range(SUB)):
            t = k * SUB + u
            row = pl.multiple_of(t * states, states)
            cc = outb[pl.ds(row, states), :]
            for g in range(groups):
                adj = cc * a_s.at[fb, lanes(g)][u:u + 1, :] + ca[g]
                hi = adj.astype(BF16)
                ab[u * states:(u + 1) * states, lanes(g)] = hi
                if lo:
                    al[u * states:(u + 1) * states, lanes(g)] = (adj - hi.astype(F32)).astype(BF16)
                ca[g] = dec_s[pl.ds(row, states), lanes(g)] * adj
                z = ca[g] * hist[pl.ds(row, states), lanes(g)]
                zr[u * states:(u + 1) * states, lanes(g)] = (z * nrate[g]).astype(BF16)
                rg[g] = rg[g] + z * d_s.at[fb, lanes(g)][u:u + 1, :]
        return ca, rg

    def bwd_mat(k, ab, al, zr):
        r32 = pl.multiple_of((k + 1) * 2 * SUB, 2 * SUB)
        r16 = pl.multiple_of((k + 1) * SUB, SUB)
        h = ab[...]
        bm = bmat[pl.ds(r32, 2 * SUB), :]
        y = jnp.dot(bm, h, preferred_element_type=F32)
        y = y[:SUB] + y[SUB:]
        if lo:
            y = y + jnp.dot(bm[:SUB], al[...], preferred_element_type=F32)
        q_s[pl.ds(r16, SUB), :] = y
        zz_s[pl.ds(r16, SUB), :] = jnp.dot(omat[...], zr[...], preferred_element_type=F32)
        o = nt(db16[pl.ds(r32, 2 * SUB), :], h)
        ic_s[pl.ds(r16, SUB), :] += o[:SUB] + o[SUB:]

    def bwd(i, carry):
        ca, rg = list(carry[0]), list(carry[1])
        k = nblk - 1 - 2 * i
        ca, rg = bwd_vec(k, ca, rg, ab0, al0, zr0)
        bwd_mat(k + 1, ab1, al1, zr1)
        ca, rg = bwd_vec(k - 1, ca, rg, ab1, al1, zr1)
        bwd_mat(k, ab0, al0, zr0)
        return tuple(ca), tuple(rg)
    z0 = tuple(jnp.zeros((states, LANES), F32) for _ in range(groups))
    _, rg = lax.fori_loop(0, nblk // 2, bwd, (tuple(a_in[:, lanes(g)] for g in range(groups)), z0))
    bwd_mat(0, ab1, al1, zr1)
    for g in range(groups):
        g_rate[:, lanes(g)] = -rg[g]

    n = tokens
    scan = ascan[SUB:SUB + n, :]
    q = q_s[SUB:SUB + n, :]
    zz = zz_s[SUB:SUB + n, :] * (1.0 / LOG2E)
    s = sig[...].astype(F32)
    g_ = gate[...].astype(F32)
    o_ = cot[...].astype(F32)
    sg = jax.nn.sigmoid(g_)
    av = a_s[...]
    k_ = skip[...]
    g_gate[...] = (o_ * (scan + k_ * s) * sg * (1.0 + g_ * (1.0 - sg))).astype(BF16)
    g_sig[...] = (d_s[...] * q + k_ * av).astype(BF16)
    rawg = (s * q + zz) * r_s[...]
    g_skip[...] = jnp.sum(s * av, 0, keepdims=True)
    g_bias[...] = jnp.sum(rawg, 0, keepdims=True)
    rr = rawg.astype(BF16)
    g_low[...] += nt(rr, w[...])
    dw[...] = lax.dot_general(low[...], rr, (((0,), (0,)), ((), ())), preferred_element_type=F32).astype(dw.dtype)

    @pl.when(step == pl.num_programs(0) - 1)
    def _():
        row = lax.broadcasted_iota(jnp.int32, (tokens, blk), 0)
        col = lax.broadcasted_iota(jnp.int32, (tokens, blk), 1)
        on = (row % SUB) == (col // states)
        pick = (lax.broadcasted_iota(jnp.int32, (blk, states), 0) % states
                == lax.broadcasted_iota(jnp.int32, (blk, states), 1)).astype(F32)
        for src, dst in ((oc_s, g_outc), (ic_s, g_inc)):
            x = jnp.where(on, src[SUB:SUB + n, :], 0.0)
            dst[...] = jnp.dot(x, pick, preferred_element_type=F32, precision=lax.Precision.HIGHEST)

WIDTH = 512

def vm(shape, dt=F32):
    return pltpu.VMEM(shape, dt)

def local_pass(low, w, bias, rate, sig, gate, cot, keep, inb, outb):
    tokens, chans = sig.shape
    n, r = rate.shape[0], low.shape[1]
    W = WIDTH
    col = lambda rows: pl.BlockSpec((rows, W), lambda j: (0, j))
    whole = lambda x: pl.BlockSpec(x.shape, lambda j: (0, 0))
    return pl.pallas_call(
        local_kernel, grid=(chans // W,),
        in_specs=[whole(low), col(r), col(1), col(n), col(tokens), col(tokens), col(tokens), whole(keep), whole(inb), whole(outb)],
        out_specs=[col(n), col(n), col(1)],
        out_shape=[jax.ShapeDtypeStruct((n, chans), F32)] * 2 + [jax.ShapeDtypeStruct((1, chans), F32)],
        scratch_shapes=[vm((tokens, W))] * 3,
        compiler_params=pltpu.CompilerParams(vmem_limit_bytes=60 << 20),
        name="local_pass",
    )(low, w, bias, rate, sig, gate, cot, keep, inb, outb)

def full_pass(low, w, bias, rate, skip, sig, gate, cot, keep, inb, outb, cmat, bmat, omat, s_in, a_in, lo=True, dwt=F32):
    tokens, chans = sig.shape
    n, r = rate.shape[0], low.shape[1]
    W = WIDTH
    blk = SUB * n
    nblk = tokens // SUB
    col = lambda rows: pl.BlockSpec((rows, W), lambda j: (0, j))
    whole = lambda x: pl.BlockSpec(x.shape, lambda j: (0, 0))
    fixed = lambda *sh: pl.BlockSpec(sh, lambda j: (0, 0))
    S = jax.ShapeDtypeStruct
    rows16, rows32 = (nblk + 2) * SUB, (nblk + 2) * 2 * SUB
    return pl.pallas_call(
        functools.partial(full_kernel, lo=lo), grid=(chans // W,),
        in_specs=[whole(low), col(r), col(1), col(n), col(1), col(tokens), col(tokens), col(tokens), whole(keep), whole(inb), whole(outb),
                  whole(cmat), whole(bmat), whole(omat), col(n), col(n)],
        out_specs=[col(tokens), col(tokens), fixed(tokens, r), fixed(tokens, n), fixed(tokens, n), col(r), col(n), col(1), col(1)],
        out_shape=[S((tokens, chans), BF16), S((tokens, chans), BF16), S((tokens, r), F32), S((tokens, n), F32), S((tokens, n), F32),
                   S((r, chans), dwt), S((n, chans), F32), S((1, chans), F32), S((1, chans), F32)],
        scratch_shapes=[vm((tokens, W))] * 5 + [vm(((tokens + 1) * n, W)), vm((tokens * n, W))] + [vm((blk, W), BF16)] * 8
            + [vm((rows16, W)), vm((rows32, W), BF16), vm((rows32, W), BF16), vm((rows16, W)), vm((rows16, W)), vm((rows16, blk)), vm((rows16, blk))],
        compiler_params=pltpu.CompilerParams(vmem_limit_bytes=60 << 20),
        name="full_pass",
    )(low, w, bias, rate, skip, sig, gate, cot, keep, inb, outb, cmat, bmat, omat, s_in, a_in)

def tables(coef_in, coef_out, keep):
    n, tokens = coef_in.shape
    nblk = tokens // SUB
    bc = lambda x: jnp.broadcast_to(x.T[:, :, None], (tokens, n, LANES)).reshape(tokens * n, LANES)
    def banded(x):
        xt = x.T
        hi = lax.reduce_precision(xt, 8, 7)
        parts = jnp.stack([hi, xt - hi])
        parts = parts.reshape(2, nblk, SUB, 1, n) * jnp.eye(SUB, dtype=F32)[None, None, :, :, None]
        m = parts.transpose(1, 0, 2, 3, 4).reshape(nblk * 2 * SUB, SUB * n)
        return jnp.pad(m, ((2 * SUB, 2 * SUB), (0, 0))).astype(BF16)
    ones = jnp.repeat(jnp.eye(SUB, dtype=F32), n, axis=1).astype(BF16)
    keepb = jnp.broadcast_to(keep[:, None], (tokens, LANES))
    return bc(coef_in), bc(coef_out), banded(coef_out), banded(coef_in), ones, keepb


def shifted(x, axis, by):
    devices = lax.axis_size(axis)
    pairs = [(i, i + by) for i in range(devices) if 0 <= i + by < devices]
    return lax.ppermute(x, axis, pairs)


def handed_on(end, total, nrate, sign):
    hops = lax.axis_size("seq")
    reach = 1
    while reach < hops:
        other, other_total = shifted((end, total), "seq", sign * reach)
        end = jnp.exp2(nrate * total) * other + end
        total = total + other_total
        reach *= 2
    return shifted(end, "seq", sign)


def shards(signal, gating, low_rank, dt_weight, dt_bias, decay_rate, skip_gain, coef_in, coef_out, segment_ids, out_grad):
    sig, gate, cot, low = signal[0], gating[0], out_grad[0], low_rank[0]
    n, owned = decay_rate.shape
    packed = jnp.concatenate([decay_rate, skip_gain[None, :], dt_bias[None, :]], 0)
    w = lax.all_gather(dt_weight, "fsdp", axis=1, tiled=True)
    params = lax.all_gather(packed, "fsdp", axis=1, tiled=True)
    rate, skip, bias = jnp.maximum(params[:-2], 1e-30), params[-2:-1], params[-1:]
    seg = segment_ids[0]
    before = shifted(seg[-1:] + 1, "seq", 1)
    prev = jnp.concatenate([before, seg[:-1] + 1])
    keep = (seg + 1 == prev).astype(F32)
    keep = keep.at[0].set(jnp.where(lax.axis_index("seq") == 0, 0.0, keep[0]))
    inb, outb, cmat, bmat, omat, keepb = tables(coef_in[0], coef_out[0], keep)
    end, back, total = local_pass(low, w, bias, rate, sig, gate, cot, keepb, inb, outb)
    nrate = rate * (-LOG2E)
    s_in = handed_on(end, total, nrate, 1)
    a_in = handed_on(back, total, nrate, -1)
    g_sig, g_gate, g_low, g_inc, g_outc, dw, g_rate, g_skip, g_bias = full_pass(
        low, w, bias, rate, skip, sig, gate, cot, keepb, inb, outb, cmat, bmat, omat, s_in, a_in, dwt=BF16)
    shares = lax.axis_size("fsdp")
    dw = lax.all_to_all(dw.reshape(-1, shares, owned), "fsdp", 1, 1)
    dw = jnp.sum(dw.astype(F32), 1)
    small = jnp.concatenate([g_rate, g_skip, g_bias], 0).reshape(n + 2, shares, owned)
    small = jnp.sum(lax.all_to_all(small, "fsdp", 1, 1), 1)
    sums = lax.psum(jnp.concatenate([dw, small], 0), "seq")
    rows = dt_weight.shape[0]
    return (g_sig[None], g_gate[None], g_low[None], g_inc.T[None], g_outc.T[None],
            sums[:rows], sums[rows:rows + n], sums[rows + n], sums[rows + n + 1])


def solution(mesh):
    return jax.shard_map(
        shards,
        mesh=mesh,
        in_specs=(
            P("fsdp", "seq", None), P("fsdp", "seq", None), P("fsdp", "seq", None),
            P(None, "fsdp"), P("fsdp"), P(None, "fsdp"), P("fsdp"),
            P("fsdp", None, "seq"), P("fsdp", None, "seq"), P("fsdp", "seq"), P("fsdp", "seq", None),
        ),
        out_specs=(
            P("fsdp", "seq", None), P("fsdp", "seq", None), P("fsdp", "seq", None),
            P("fsdp", None, "seq"), P("fsdp", None, "seq"), P(None, "fsdp"), P(None, "fsdp"), P("fsdp"), P("fsdp"),
        ),
        check_vma=False,
    )
```

time: 1880 us -> 584 us (0.31); the launches traced: 1850 us -> 582 us
  other arithmetic: 994 us -> 16 us
  local copies, waits for them, and re-layouts: 286 us -> 28.1 us
  Pallas kernels: 0 us -> 162 us
  waiting for transfers between devices: 383 us -> 273 us
  blocking collectives: 64.7 us -> 21.5 us
  loops' own time: 28.8 us -> 0 us
  matrix products: 25.3 us -> 0 us
    reduce_sum x75 -> x2, other arithmetic: 383 us -> 4.75 us  [the longest x1 4.69 us: shards(): dw = jnp.sum(dw.astype(F32), 1)]
    pallas_call x0 -> x2, Pallas kernels: none -> 162 us  [the longest x1 125 us: full_pass(): pl.pallas_call(functools.partial(full_kernel, lo=lo), grid=(chans // W,),...]
    mul x40 -> x5, other arithmetic: 162 us -> 1.01 us  [the longest x3 0.98 us: handed_on(): end = jnp.exp2(nrate * total) * other + end]
    add x63 -> x4, other arithmetic: 160 us -> 3.62 us  [the longest x3 2.96 us: handed_on(): end = jnp.exp2(nrate * total) * other + end]
    reduce_scatter x2 -> x0, waiting for transfers between devices: 149 us -> none  [the longest x1 105 us: shards(): lax.psum_scatter(weight_part, 'fsdp', scatter_dimension=1, tiled=True)]
    sub x9 -> x0, other arithmetic: 138 us -> none  [the longest x8 137 us: full_block(): rate_grad - adj * prior * decays[offset] * d_blk[offset][None, :]]
    ppermute x15 -> x13, waiting for transfers between devices: 169 us -> 38.6 us  [shifted(): return lax.ppermute(x, axis, pairs)]
    neg x121 -> x0, other arithmetic: 128 us -> none  [the longest x120 126 us: decay_of(): return jnp.exp(-d_row[None, :] * rate_all) * k_val]
  transfers between devices with their start and end apart: 19 -> 17, of which waited for: 18 -> 11; matrix products, arithmetic and copies ran while one was open for 2% -> 4% of each run, Pallas kernels for 0% -> 0%
where the time goes in v1:
time: 584 us; the launch traced here: 582 us
  waiting for transfers between devices  273 us (47%)
  Pallas kernels  162 us (28%)
  starting transfers between devices  66.5 us (11%)
  local copies, waits for them, and re-layouts  28.1 us (5%)
  blocking collectives  21.5 us (4%)
  other arithmetic  16 us (3%)
  between operations  15.1 us (3%)
    pallas_call x1, Pallas kernels, full_pass(): pl.pallas_call(functools.partial(full_kernel, lo=lo), grid=(chans // W,),...  125 us
    all_to_all x1, waiting for transfers between devices, shards(): dw = lax.all_to_all(dw.reshape(-1, shares, owned), 'fsdp', 1, 1)  111 us
    psum x1, waiting for transfers between devices, shards(): sums = lax.psum(jnp.concatenate([dw, small], 0), 'seq')  96.2 us
    ppermute x13, starting transfers between devices, shifted(): return lax.ppermute(x, axis, pairs)  52.7 us
    ppermute x13, waiting for transfers between devices, shifted(): return lax.ppermute(x, axis, pairs)  38.6 us
    pallas_call x1, Pallas kernels, local_pass(): pl.pallas_call(local_kernel, grid=(chans // W,), in_specs=[whole(low), co...  37.6 us
    all_gather x1, waiting for transfers between devices, shards(): w = lax.all_gather(dt_weight, 'fsdp', axis=1, tiled=True)  23.9 us
    all_gather x1, blocking collectives, shards(): params = lax.all_gather(packed, 'fsdp', axis=1, tiled=True)  21.5 us
  transfers between devices with their start and end apart: 17, of which 11 were waited for; matrix products, arithmetic and copies ran while one was open for 4% of the time, Pallas kernels for 0%

profile of v1, /device:TPU:4, one launch (start us, length us, event | category | flops | bytes accessed | tf_op | source)
XLA Modules:
  0.0 582.4 jit_solution(8454961045989986914)
XLA Ops:
  7.2 0.7 all-gather.2.cloned.1.call-update
  7.9 1.2 slice.45
  9.8 5.1 collective-permute-start
  14.9 0.7 bitcast_reduce-precision_fusion.1
  15.8 0.8 copy.31
  16.7 0.8 copy.30
  17.5 0.8 pad_maximum_fusion.2
  18.4 0.7 add_bitcast_fusion
  19.0 0.7 bitcast_reduce-precision_fusion
  19.7 21.5 %all_gather.7 = f32[18,8192]{1,0:T(8,128)S(1)} all-gather(f32[18,512]{1,0:T(8,128)S(1)} %pad_maximum_fusion.2), channel_id=1, replica_groups=mesh['seq'=8,'fsdp'=16] {'fsdp'}, dimensions={1}, use_global_device_ids=true | all-gather | bytes 626688 | tf_op jit(solution)/shard_map/all_gather | solution.py:289
  41.2 0.7 fusion.3
  41.9 0.9 slice_maximum_fusion.rate
  42.7 0.8 compare_convert_fusion
  43.6 23.9 %all-gather.2.cloned.1.call-done.w = bf16[512,8192]{1,0:T(8,128)(2,1)} async-done(((bf16[512,512]{1,0:T(8,128)(2,1)}), bf16[512,8192]{1,0:T(8,128)(2,1)}) %all-gather.2.cloned.1.call-update) | async-done | bytes 8388624 | tf_op jit(solution)/shard_map/all_gather | solution.py:288
  67.4 0.7 broadcast_in_dim.53.keep
  68.1 1.3 broadcast_in_dim.55.inb
  69.4 1.3 broadcast_in_dim.57.outb
  70.8 37.6 %local_pass.1 = (f32[16,8192]{1,0:T(8,128)}, f32[16,8192]{1,0:T(8,128)}, f32[1,8192]{1,0:T(1,128)}) custom-call(bf16[128,512]{1,0:T(8,128)(2,1)} %bitcast.77, bf16[512,8192]{1,0:T(8,128)(2,1)} %all-gather.2.cloned.1.call-done.w, f32[1,8192]{1,0:T(1,128)} %get-tuple-element.85.bias, f32[16,8192]{1,0:T(8,128)} %slice_maximum_fusion.rate, ...), custom_call_target="tpu_custom_call" | custom-call | tf_op jit(solution)/shard_map/local_pass/pallas_call | solution.py:217
  108.4 1.3 collective-permute-start.7
  109.7 4.5 collective-permute-start.1
  114.3 3.5 collective-permute-start.3
  117.8 1.3 collective-permute-start.9
  119.1 0.9 broadcast_multiply_fusion
  120.0 1.3 collective-permute-start.8
  121.3 9.6 %collective-permute-start.2 = (f32[1,8192]{1,0:T(1,128)S(1)}, f32[1,8192]{1,0:T(1,128)S(1)}, u32[]{:S(2)}, u32[]{:S(2)}) collective-permute-start(f32[1,8192]{1,0:T(1,128)S(1)} %get-tuple-element.88), channel_id=1, source_target_pairs={{0,32},{16,48},{32,64},{48,80},{64,96},{80,112},{1,33},{17,49},{33... | collective-permute-start | bytes 98312 | tf_op jit(solution)/shard_map/ppermute | solution.py:270
  130.9 2.9 collective-permute-done.9
  133.8 1.4 multiply_add_fusion.2
  135.3 1.3 collective-permute-start.10
  136.6 8.7 %collective-permute-start.4 = (f32[16,8192]{1,0:T(8,128)S(1)}, f32[16,8192]{1,0:T(8,128)S(1)}, u32[]{:S(2)}, u32[]{:S(2)}) collective-permute-start(f32[16,8192]{1,0:T(8,128)S(1)} %get-tuple-element.79), channel_id=1, source_target_pairs={{0,32},{16,48},{32,64},{48,80},{64,96},{80,112},{1,33},{17,49},{33... | collective-permute-start | bytes 1572872 | tf_op jit(solution)/shard_map/ppermute | solution.py:270
  145.3 8.2 %collective-permute-done.10 = f32[16,8192]{1,0:T(8,128)S(1)} collective-permute-done((f32[16,8192]{1,0:T(8,128)S(1)}, f32[16,8192]{1,0:T(8,128)S(1)}, u32[]{:S(2)}, u32[]{:S(2)}) %collective-permute-start.10) | collective-permute-done | bytes 524320 | tf_op jit(solution)/shard_map/ppermute | solution.py:270
  153.5 12.4 %collective-permute-done.4 = f32[16,8192]{1,0:T(8,128)S(1)} collective-permute-done((f32[16,8192]{1,0:T(8,128)S(1)}, f32[16,8192]{1,0:T(8,128)S(1)}, u32[]{:S(2)}, u32[]{:S(2)}) %collective-permute-start.4) | collective-permute-done | bytes 524320 | tf_op jit(solution)/shard_map/ppermute | solution.py:270
  166.2 1.3 collective-permute-start.11
  167.5 6.1 %collective-permute-start.5 = (f32[16,8192]{1,0:T(8,128)S(1)}, f32[16,8192]{1,0:T(8,128)S(1)}, u32[]{:S(2)}, u32[]{:S(2)}) collective-permute-start(f32[16,8192]{1,0:T(8,128)S(1)} %get-tuple-element.83), channel_id=1, source_target_pairs={{0,64},{16,80},{32,96},{48,112},{1,65},{17,81},{33,97},{49,113},{2... | collective-permute-start | bytes 1572872 | tf_op jit(solution)/shard_map/ppermute | solution.py:270
  173.7 9.2 %collective-permute-done.11 = f32[16,8192]{1,0:T(8,128)S(1)} collective-permute-done((f32[16,8192]{1,0:T(8,128)S(1)}, f32[16,8192]{1,0:T(8,128)S(1)}, u32[]{:S(2)}, u32[]{:S(2)}) %collective-permute-start.11) | collective-permute-done | bytes 524320 | tf_op jit(solution)/shard_map/ppermute | solution.py:270
  182.9 1.2 collective-permute-done.5
  184.1 1.2 multiply_add_fusion
  185.3 1.3 collective-permute-start.12
  186.6 7.5 %collective-permute-start.6 = (f32[16,8192]{1,0:T(8,128)}, f32[16,8192]{1,0:T(8,128)S(1)}, u32[]{:S(2)}, u32[]{:S(2)}) collective-permute-start(f32[16,8192]{1,0:T(8,128)} %get-tuple-element.81), channel_id=1, source_target_pairs={{0,16},{16,32},{32,48},{48,64},{64,80},{80,96},{96,112},{1,17},{17... | collective-permute-start | bytes 1572872 | tf_op jit(solution)/shard_map/ppermute | solution.py:270
  194.3 0.7 convert_element_type.36.omat
  195.3 0.6 multiply_convert_fusion
  196.0 1.0 mul.140
  196.9 1.0 mul.135
  197.9 0.7 pad.12.bmat
  198.6 0.7 pad.11.cmat
  199.3 3.4 collective-permute-done.12.a_in
  202.7 1.3 collective-permute-done.6.s_in
  204.0 0.8 copy-done.1
  204.8 124.5 %full_pass.1 = (bf16[128,8192]{1,0:T(8,128)(2,1)}, bf16[128,8192]{1,0:T(8,128)(2,1)}, f32[128,512]{1,0:T(8,128)}, f32[128,16]{1,0:T(8,128)}, f32[128,16]{1,0:T(8...) custom-call(bf16[128,512]{1,0:T(8,128)(2,1)} %bitcast.78, ...), custom_call_target="tpu_custom_call" | custom-call | tf_op jit(solution)/shard_map/full_pass/pallas_call | solution.py:238
  329.3 1.2 pad_maximum_fusion.1
  330.4 0.5 copy.39
  331.0 1.2 copy.35
  332.2 5.6 all-to-all-start.1
  337.8 7.6 %copy.41 = bf16[64,16,8,512]{3,2,0,1:T(8,128)(2,1)} copy(bf16[64,16,8,512]{3,2,1,0:T(8,128)(2,1)} %bitcast.74) | data formatting | bytes 16777216 | tf_op jit(solution)/shard_map/reshape | solution.py:304
  345.4 2.8 all-to-all-done.1
  348.2 8.0 %all-to-all-start = ((bf16[512,16,512]{2,0,1:T(8,128)(2,1)}), bf16[512,16,512]{2,0,1:T(8,128)(2,1)}, u32[]{:S(2)}, u32[]{:S(2)}) async-start(bf16[512,16,512]{2,0,1:T(8,128)(2,1)} %bitcast.67), calls=%async_computation | async-start | bytes 16777216 | tf_op jit(solution)/shard_map/all_to_all | solution.py:304
  356.3 110.9 %all-to-all-done = bf16[512,16,512]{2,0,1:T(8,128)(2,1)} async-done(((bf16[512,16,512]{2,0,1:T(8,128)(2,1)}), bf16[512,16,512]{2,0,1:T(8,128)(2,1)}, u32[]{:S(2)}, u32[]{:S(2)}) %all-to-all-start) | async-done | bytes 8388640 | tf_op jit(solution)/shard_map/all_to_all | solution.py:304
  467.2 4.7 convert_reduce_fusion
  471.9 1.0 pad_maximum_fusion
  473.0 0.7 copy.36
  473.7 0.7 copy.37
  474.3 96.2 %all-reduce.4.cloned.1.call-done = f32[530,512]{1,0:T(8,128)} async-done(((f32[530,512]{1,0:T(8,128)}), f32[530,512]{1,0:T(8,128)}) %all-reduce.4.cloned.1.call-update) | async-done | bytes 1085456 | tf_op jit(solution)/shard_map/psum | solution.py:308
  570.6 1.4 fusion.2
  571.9 1.4 slice.56
  573.3 2.3 slice.55
  (37 shorter events, 1.4 us)
Async XLA Ops:
  7.2 35.6 %copy-start.4 = (s32[1,128]{1,0:T(1,128)S(1)}, s32[1,128]{1,0:T(1,128)}, u32[]{:S(2)}) copy-start(s32[1,128]{1,0:T(1,128)} %param.22) | copy-start | bytes 1540
  7.2 60.2 %all-gather.2.cloned.1.call-start = ((), (), s32[]{:S(2)}) async-start(), calls=%async_computation.2 | async-start | bytes 8912896 | tf_op jit(solution)/shard_map/all_gather | solution.py:288
  9.8 32.9 %collective-permute-start = (s32[1]{0:T(128)}, s32[1]{0:T(128)}, u32[]{:S(2)}, u32[]{:S(2)}) collective-permute-start(s32[1]{0:T(128)} %bitcast.7), channel_id=1, source_target_pairs={{0,16},{16,32},{32,48},{48,64},{64,80},{80,96},{96,112},{1,17},{17... | collective-permute-start | bytes 20 | tf_op jit(solution)/shard_map/ppermute | solution.py:270
  108.4 10.7 %collective-permute-start.7 = (f32[1,8192]{1,0:T(1,128)}, f32[1,8192]{1,0:T(1,128)S(1)}, u32[]{:S(2)}, u32[]{:S(2)}) collective-permute-start(f32[1,8192]{1,0:T(1,128)} %get-tuple-element.33), channel_id=1, source_target_pairs={{16,0},{32,16},{48,32},{64,48},{80,64},{96,80},{112,96},{17,1},{33... | collective-permute-start | bytes 98312 | tf_op jit(solution)/shard_map/ppermute | solution.py:270
  109.7 9.4 %collective-permute-start.1 = (f32[1,8192]{1,0:T(1,128)}, f32[1,8192]{1,0:T(1,128)S(1)}, u32[]{:S(2)}, u32[]{:S(2)}) collective-permute-start(f32[1,8192]{1,0:T(1,128)} %get-tuple-element.33), channel_id=1, source_target_pairs={{0,16},{16,32},{32,48},{48,64},{64,80},{80,96},{96,112},{1,17},{17... | collective-permute-start | bytes 98312 | tf_op jit(solution)/shard_map/ppermute | solution.py:270
  114.3 16.6 %collective-permute-start.3 = (f32[16,8192]{1,0:T(8,128)}, f32[16,8192]{1,0:T(8,128)S(1)}, u32[]{:S(2)}, u32[]{:S(2)}) collective-permute-start(f32[16,8192]{1,0:T(8,128)} %get-tuple-element.34), channel_id=1, source_target_pairs={{0,16},{16,32},{32,48},{48,64},{64,80},{80,96},{96,112},{1,17},{17... | collective-permute-start | bytes 1572872 | tf_op jit(solution)/shard_map/ppermute | solution.py:270
  117.8 16.0 %collective-permute-start.9 = (f32[16,8192]{1,0:T(8,128)}, f32[16,8192]{1,0:T(8,128)S(1)}, u32[]{:S(2)}, u32[]{:S(2)}) collective-permute-start(f32[16,8192]{1,0:T(8,128)} %get-tuple-element.35), channel_id=1, source_target_pairs={{16,0},{32,16},{48,32},{64,48},{80,64},{96,80},{112,96},{17,1},{33... | collective-permute-start | bytes 1572872 | tf_op jit(solution)/shard_map/ppermute | solution.py:270
  120.0 25.2 %collective-permute-start.8 = (f32[1,8192]{1,0:T(1,128)S(1)}, f32[1,8192]{1,0:T(1,128)S(1)}, u32[]{:S(2)}, u32[]{:S(2)}) collective-permute-start(f32[1,8192]{1,0:T(1,128)S(1)} %get-tuple-element.73), channel_id=1, source_target_pairs={{32,0},{48,16},{64,32},{80,48},{96,64},{112,80},{33,1},{49,17},{65... | collective-permute-start | bytes 98312 | tf_op jit(solution)/shard_map/ppermute | solution.py:270
  121.3 52.3 %collective-permute-start.2 = (f32[1,8192]{1,0:T(1,128)S(1)}, f32[1,8192]{1,0:T(1,128)S(1)}, u32[]{:S(2)}, u32[]{:S(2)}) collective-permute-start(f32[1,8192]{1,0:T(1,128)S(1)} %get-tuple-element.88), channel_id=1, source_target_pairs={{0,32},{16,48},{32,64},{48,80},{64,96},{80,112},{1,33},{17,49},{33... | collective-permute-start | bytes 98312 | tf_op jit(solution)/shard_map/ppermute | solution.py:270
  135.3 18.2 %collective-permute-start.10 = (f32[16,8192]{1,0:T(8,128)S(1)}, f32[16,8192]{1,0:T(8,128)S(1)}, u32[]{:S(2)}, u32[]{:S(2)}) collective-permute-start(f32[16,8192]{1,0:T(8,128)S(1)} %get-tuple-element.78), channel_id=1, source_target_pairs={{32,0},{48,16},{64,32},{80,48},{96,64},{112,80},{33,1},{49,17},{65... | collective-permute-start | bytes 1572872 | tf_op jit(solution)/shard_map/ppermute | solution.py:270
  136.6 29.3 %collective-permute-start.4 = (f32[16,8192]{1,0:T(8,128)S(1)}, f32[16,8192]{1,0:T(8,128)S(1)}, u32[]{:S(2)}, u32[]{:S(2)}) collective-permute-start(f32[16,8192]{1,0:T(8,128)S(1)} %get-tuple-element.79), channel_id=1, source_target_pairs={{0,32},{16,48},{32,64},{48,80},{64,96},{80,112},{1,33},{17,49},{33... | collective-permute-start | bytes 1572872 | tf_op jit(solution)/shard_map/ppermute | solution.py:270
  166.2 16.7 %collective-permute-start.11 = (f32[16,8192]{1,0:T(8,128)S(1)}, f32[16,8192]{1,0:T(8,128)S(1)}, u32[]{:S(2)}, u32[]{:S(2)}) collective-permute-start(f32[16,8192]{1,0:T(8,128)S(1)} %get-tuple-element.82), channel_id=1, source_target_pairs={{64,0},{80,16},{96,32},{112,48},{65,1},{81,17},{97,33},{113,49},{6... | collective-permute-start | bytes 1572872 | tf_op jit(solution)/shard_map/ppermute | solution.py:270
  167.5 16.6 %collective-permute-start.5 = (f32[16,8192]{1,0:T(8,128)S(1)}, f32[16,8192]{1,0:T(8,128)S(1)}, u32[]{:S(2)}, u32[]{:S(2)}) collective-permute-start(f32[16,8192]{1,0:T(8,128)S(1)} %get-tuple-element.83), channel_id=1, source_target_pairs={{0,64},{16,80},{32,96},{48,112},{1,65},{17,81},{33,97},{49,113},{2... | collective-permute-start | bytes 1572872 | tf_op jit(solution)/shard_map/ppermute | solution.py:270
  185.3 17.4 %collective-permute-start.12 = (f32[16,8192]{1,0:T(8,128)}, f32[16,8192]{1,0:T(8,128)S(1)}, u32[]{:S(2)}, u32[]{:S(2)}) collective-permute-start(f32[16,8192]{1,0:T(8,128)} %get-tuple-element.80), channel_id=1, source_target_pairs={{16,0},{32,16},{48,32},{64,48},{80,64},{96,80},{112,96},{17,1},{33... | collective-permute-start | bytes 1572872 | tf_op jit(solution)/shard_map/ppermute | solution.py:270
  186.6 17.4 %collective-permute-start.6 = (f32[16,8192]{1,0:T(8,128)}, f32[16,8192]{1,0:T(8,128)S(1)}, u32[]{:S(2)}, u32[]{:S(2)}) collective-permute-start(f32[16,8192]{1,0:T(8,128)} %get-tuple-element.81), channel_id=1, source_target_pairs={{0,16},{16,32},{32,48},{48,64},{64,80},{80,96},{96,112},{1,17},{17... | collective-permute-start | bytes 1572872 | tf_op jit(solution)/shard_map/ppermute | solution.py:270
  202.7 1.3 copy-start
  204.0 0.8 copy-start.1
  332.2 16.0 %all-to-all-start.1 = ((f32[18,16,512]{2,0,1:T(8,128)}), f32[18,16,512]{2,0,1:T(8,128)S(1)}, u32[]{:S(2)}, u32[]{:S(2)}) async-start(f32[18,16,512]{2,0,1:T(8,128)} %copy.35), calls=%async_computation.1 | async-start | bytes 1572864 | tf_op jit(solution)/shard_map/all_to_all | solution.py:307
  348.2 119.1 %all-to-all-start = ((bf16[512,16,512]{2,0,1:T(8,128)(2,1)}), bf16[512,16,512]{2,0,1:T(8,128)(2,1)}, u32[]{:S(2)}, u32[]{:S(2)}) async-start(bf16[512,16,512]{2,0,1:T(8,128)(2,1)} %bitcast.67), calls=%async_computation | async-start | bytes 16777216 | tf_op jit(solution)/shard_map/all_to_all | solution.py:304
  356.2 214.4 %all-reduce.4.cloned.1.call-start = ((), (), s32[]{:S(2)}) async-start(), calls=%async_computation.3 | async-start | bytes 2195456 | tf_op jit(solution)/shard_map/psum | solution.py:308
  471.9 1.1 copy-start.3
  471.9 1.8 copy-start.2
Sparse Core Ops, SparseCore 0:
  9.7 57.7 all-gather.1
  473.1 97.3 all-reduce.3

commit v2 on v0

v2 whole, which is shorter than its diff:
```python
import functools, math
import jax, jax.numpy as jnp
from jax import lax
from jax.experimental import pallas as pl
from jax.experimental.pallas import tpu as pltpu
from jax.sharding import PartitionSpec as P

F32, BF16 = jnp.float32, jnp.bfloat16
LANES = 128
SUB = 16
LOG2E = math.log2(math.e)

PEERS = 7
PAIRS = 8
ROWS = 24
MESH = pl.DeviceIdType.MESH


def nt(x, y):
    return lax.dot_general(x, y, (((1,), (1,)), ((), ())), preferred_element_type=F32)


def wide(x, width):
    return jnp.concatenate([x] * (width // LANES), 1)


def softplus(x):
    return jnp.maximum(x, 0.0) + jnp.log1p(jnp.exp(-jnp.abs(x)))


def kernel(low, w_own, par_own, sig, gate, cot, keepb, segb, inb, outb, cmat, bmat, omat,
           g_sig, g_gate, g_low, g_inc, g_outc, g_w, g_small,
           wall, pall, lowt, keep_s, seg_in, xs, er,
           dk_s, d_s, ds_s, a_s, r_s, hist, dec_s, hb0, hb1, ab0, ab1, al0, al1, zr0, zr1,
           scan_s, a16, d16, q_s, zz_s, oc_s, ic_s,
           bsend, brecv, bsmall, brsmall, astage, asmall, drecv, srecv, acc, accs, rs, rss, fin,
           w_ss, w_rs, p_ss, p_rs, wf_ss, wf_rs, pf_ss, pf_rs, x_ss, x_rs, b_ss, b_rs, bs_ss, bs_rs,
           d_ss, d_rs, s_ss, s_rs, r_ss, r_rs, t_ss, t_rs, f_ss, f_rs, seg_ss, seg_rs, own_sem, credit):
    tokens = low.shape[0]
    width = w_own.shape[1]
    states = outb.shape[0] // tokens
    blk = SUB * states
    nblk = tokens // SUB
    seq = lax.axis_index("seq")
    me = lax.axis_index("fsdp")
    chip, core = me // 2, me % 2
    cy, cx = chip // 4, chip % 4
    sibling = (seq, chip * 2 + (1 - core))

    def target(k):
        return (seq, (((cy + k // 4) % 2) * 4 + (cx + k % 4) % 4) * 2 + core)

    def source_chip(k):
        return ((cy + k // 4) % 2) * 4 + (cx + 4 - k % 4) % 4

    def peer(i):
        return ((seq + i) % 8, me)

    def remote(src, dst, ss, rs_, dev):
        return pltpu.make_async_remote_copy(src_ref=src, dst_ref=dst, send_sem=ss, recv_sem=rs_, device_id=dev, device_id_type=MESH)

    barrier = pltpu.get_barrier_semaphore()
    for k in range(1, PAIRS):
        pl.semaphore_signal(barrier, inc=1, device_id=target(k), device_id_type=MESH)
    for i in range(1, PEERS + 1):
        pl.semaphore_signal(barrier, inc=1, device_id=peer(i), device_id_type=MESH)
    pl.semaphore_signal(barrier, inc=1, device_id=sibling, device_id_type=MESH)
    pl.semaphore_wait(barrier, PAIRS + PEERS)

    def push_w(k):
        return (remote(w_own, wall.at[2 * k], w_ss.at[k], w_rs.at[k], target(k)),
                remote(par_own, pall.at[2 * k], p_ss.at[k], p_rs.at[k], target(k)))

    def forward_w(k):
        return (remote(wall.at[2 * k], wall.at[2 * k + 1], wf_ss.at[k], wf_rs.at[k], sibling),
                remote(pall.at[2 * k], pall.at[2 * k + 1], pf_ss.at[k], pf_rs.at[k], sibling))

    def send_seg():
        return remote(segb, seg_in, seg_ss, seg_rs, peer(1))

    send_seg().start()
    for k in range(1, 4):
        for c in push_w(k):
            c.start()
    own = (pltpu.make_async_copy(w_own, wall.at[0], own_sem.at[0]), pltpu.make_async_copy(par_own, pall.at[0], own_sem.at[1]))
    for c in own:
        c.start()
    lowt[...] = low[...].T
    oc_s[...] = jnp.zeros_like(oc_s)
    ic_s[...] = jnp.zeros_like(ic_s)
    g_low[...] = jnp.zeros_like(g_low)
    for c in own:
        c.wait()
    send_seg().wait_recv()
    keep_s[...] = keepb[...]
    same = jnp.where(seg_in[SUB // 2:SUB // 2 + 1, :] == segb[0:1, :], 1.0, 0.0)
    keep_s[0:1, :] = jnp.where(seq == 0, 0.0, same)

    def columns(k, other):
        return pl.ds(pl.multiple_of((source_chip(k) * 2 + (core if other == 0 else 1 - core)) * width, width), width)

    def prepare(slot, cols):
        raw = jnp.dot(low[...], wall[slot], preferred_element_type=F32) + pall[slot, states + 1:states + 2, :]
        delta = softplus(raw)
        g = gate[:, cols].astype(F32)
        a = cot[:, cols].astype(F32) * g * jax.nn.sigmoid(g)
        dk_s[...] = jnp.where(wide(keep_s[...], width) > 0, delta, jnp.inf)
        ds = delta * sig[:, cols].astype(F32)
        ds_s[...] = ds
        a_s[...] = a
        return raw, delta, ds, a

    def rates(slot):
        return pall[slot, 0:states, :] * (-LOG2E)

    def block(i):
        return pl.ds(pl.multiple_of(i * SUB, SUB), SUB)

    def coef(ref, t):
        return wide(ref[pl.ds(pl.multiple_of(t * states, states), states), :], width)

    def local_pass(slot, cols, up, down):
        prepare(slot, cols)
        nrate = rates(slot)

        def body(i, carry):
            st, ad = carry
            for u in range(SUB):
                t = i * SUB + u
                d1 = dk_s.at[block(i), :]
                d2 = dk_s.at[block(nblk - 1 - i), :]
                v = SUB - 1 - u
                st = jnp.exp2(nrate * d1[u:u + 1, :]) * st + coef(inb, t) * ds_s.at[block(i), :][u:u + 1, :]
                ad = jnp.exp2(nrate * d2[v:v + 1, :]) * (coef(outb, tokens - 1 - t) * a_s.at[block(nblk - 1 - i), :][v:v + 1, :] + ad)
            return st, ad
        zero = jnp.zeros((states, width), F32)
        st, ad = lax.fori_loop(0, nblk, body, (zero, zero))
        total = jnp.broadcast_to(jnp.sum(dk_s[...], 0, keepdims=True), (ROWS - states, width))
        up[0:states, :] = st
        up[states:ROWS, :] = total
        down[0:states, :] = ad
        down[states:ROWS, :] = total

    def send_ends(k, i):
        return remote(xs.at[k, (seq + i) // 8], er.at[k, i - 1], x_ss.at[k, i - 1], x_rs.at[k, i - 1], peer(i))

    def first(k, carry):
        @pl.when(k > 0)
        def _():
            for c in push_w(k):
                c.wait_recv()
        for c in forward_w(k):
            c.start()

        @pl.when((k > 0) & (k < PAIRS - 3))
        def _():
            for c in push_w(k + 3):
                c.start()
        local_pass(2 * k, columns(k, 0), xs.at[k, 0, pl.ds(0, ROWS)], xs.at[k, 1, pl.ds(0, ROWS)])
        for c in forward_w(k):
            c.wait_recv()
        local_pass(2 * k + 1, columns(k, 1), xs.at[k, 0, pl.ds(ROWS, ROWS)], xs.at[k, 1, pl.ds(ROWS, ROWS)])
        for i in range(1, PEERS + 1):
            send_ends(k, i).start()
        return carry
    lax.fori_loop(0, PAIRS, first, 0)

    def entering(k, base, nrate):
        st = jnp.zeros((states, width), F32)
        ad = jnp.zeros((states, width), F32)
        for i in range(PEERS, 0, -1):
            e = er.at[k, i - 1]
            st = jnp.where(seq >= i, jnp.exp2(nrate * e[base + states:base + states + 1, :]) * st + e[base:base + states, :], st)
            e = er.at[k, PEERS - i]
            ad = jnp.where(seq + i < 8, jnp.exp2(nrate * e[base + states:base + states + 1, :]) * ad + e[base:base + states, :], ad)
        return st, ad

    def split(ref, x):
        hi = x.astype(BF16)
        rest = (x - hi.astype(F32)).astype(BF16)
        for b in range(nblk):
            ref[2 * SUB * (b + 1):2 * SUB * (b + 1) + SUB, :] = hi[b * SUB:(b + 1) * SUB]
            ref[2 * SUB * (b + 1) + SUB:2 * SUB * (b + 2), :] = rest[b * SUB:(b + 1) * SUB]

    def both(x):
        return x[:SUB] + x[SUB:]

    def full_pass(k, slot, cols, base, small):
        raw, delta, ds, a = prepare(slot, cols)
        d_s[...] = delta
        r_s[...] = jax.nn.sigmoid(raw)
        split(a16, a)
        split(d16, ds)
        nrate = rates(slot)
        st0, ad0 = entering(k, base, nrate)
        hist[0:states, :] = st0

        def fwd_vec(b, st, hb):
            for u in range(SUB):
                row = pl.multiple_of((b * SUB + u) * states, states)
                dec = jnp.exp2(nrate * dk_s.at[block(b), :][u:u + 1, :])
                dec_s[pl.ds(row, states), :] = dec
                st = dec * st + coef(inb, b * SUB + u) * ds_s.at[block(b), :][u:u + 1, :]
                hist[pl.ds(row + states, states), :] = st
                hb[u * states:(u + 1) * states, :] = st.astype(BF16)
            return st

        def rows(b, size):
            return pl.ds(pl.multiple_of((b + 1) * size, size), size)

        def fwd_mat(b, hb):
            h = hb[...]
            scan_s[rows(b, SUB), :] = both(jnp.dot(cmat[rows(b, 2 * SUB), :], h, preferred_element_type=F32))
            oc_s[rows(b, SUB), :] += both(nt(a16[rows(b, 2 * SUB), :], h))

        def fwd(i, st):
            st = fwd_vec(2 * i, st, hb0)
            fwd_mat(2 * i - 1, hb1)
            st = fwd_vec(2 * i + 1, st, hb1)
            fwd_mat(2 * i, hb0)
            return st
        lax.fori_loop(0, nblk // 2, fwd, st0)
        fwd_mat(nblk - 1, hb1)

        def bwd_vec(b, ca, rg, ab, al, zr):
            for u in reversed(range(SUB)):
                row = pl.multiple_of((b * SUB + u) * states, states)
                adj = coef(outb, b * SUB + u) * a_s.at[block(b), :][u:u + 1, :] + ca
                hi = adj.astype(BF16)
                ab[u * states:(u + 1) * states, :] = hi
                al[u * states:(u + 1) * states, :] = (adj - hi.astype(F32)).astype(BF16)
                ca = dec_s[pl.ds(row, states), :] * adj
                z = ca * hist[pl.ds(row, states), :]
                zr[u * states:(u + 1) * states, :] = (z * nrate).astype(BF16)
                rg = rg + z * d_s.at[block(b), :][u:u + 1, :]
            return ca, rg

        def bwd_mat(b, ab, al, zr):
            h = ab[...]
            bm = bmat[rows(b, 2 * SUB), :]
            q_s[rows(b, SUB), :] = (both(jnp.dot(bm, h, preferred_element_type=F32))
                                    + jnp.dot(bm[:SUB], al[...], preferred_element_type=F32))
            zz_s[rows(b, SUB), :] = jnp.dot(omat[...], zr[...], preferred_element_type=F32)
            ic_s[rows(b, SUB), :] += both(nt(d16[rows(b, 2 * SUB), :], h))

        def bwd(i, carry):
            b = nblk - 1 - 2 * i
            carry = bwd_vec(b, *carry, ab0, al0, zr0)
            bwd_mat(b + 1, ab1, al1, zr1)
            carry = bwd_vec(b - 1, *carry, ab1, al1, zr1)
            bwd_mat(b, ab0, al0, zr0)
            return carry
        _, rg = lax.fori_loop(0, nblk // 2, bwd, (ad0, jnp.zeros((states, width), F32)))
        bwd_mat(0, ab1, al1, zr1)

        q = q_s[SUB:SUB + tokens, :]
        s = sig[:, cols].astype(F32)
        g = gate[:, cols].astype(F32)
        o = cot[:, cols].astype(F32)
        sg = jax.nn.sigmoid(g)
        av = a_s[...]
        gain = pall[slot, states:states + 1, :]
        g_gate[:, cols] = (o * (scan_s[SUB:SUB + tokens, :] + gain * s) * sg * (1.0 + g * (1.0 - sg))).astype(BF16)
        g_sig[:, cols] = (d_s[...] * q + gain * av).astype(BF16)
        rawg = (s * q + zz_s[SUB:SUB + tokens, :] * (1.0 / LOG2E)) * r_s[...]
        small[0:states, :] = -rg
        small[states:ROWS, :] = jnp.zeros((ROWS - states, width), F32)
        small[states:states + 1, :] = jnp.sum(s * av, 0, keepdims=True)
        small[states + 1:states + 2, :] = jnp.sum(rawg, 0, keepdims=True)
        rr = rawg.astype(BF16)
        g_low[...] += nt(rr, wall[slot])
        return jnp.dot(lowt[...], rr, preferred_element_type=F32)

    def to_sibling(k):
        return (remote(bsend.at[k % 2], brecv.at[k % 2], b_ss.at[k], b_rs.at[k], sibling),
                remote(bsmall.at[k % 2], brsmall.at[k % 2], bs_ss.at[k], bs_rs.at[k], sibling))

    def to_owner(k):
        dev = (seq, source_chip(k) * 2 + core)
        return (remote(astage.at[k % 2], drecv.at[k - 1], d_ss.at[k], d_rs.at[k], dev),
                remote(asmall.at[k % 2], srecv.at[k - 1], s_ss.at[k], s_rs.at[k], dev))

    def second(m, carry):
        k = (m + 1) % PAIRS
        for i in range(1, PEERS + 1):
            send_ends(k, i).wait_recv()

        @pl.when(m >= 2)
        def _():
            for c in to_sibling(m - 1):
                c.wait_send()
            pl.semaphore_wait(credit, 1)
        bsend[k % 2] = full_pass(k, 2 * k + 1, columns(k, 1), ROWS, bsmall.at[k % 2])
        for c in to_sibling(k):
            c.start()

        @pl.when((m >= 2) & (m < PAIRS - 1))
        def _():
            for c in to_owner(m - 1):
                c.wait_send()
        acc[...] = full_pass(k, 2 * k, columns(k, 0), 0, accs)
        for c in to_sibling(k):
            c.wait_recv()
        acc[...] += brecv[k % 2]
        accs[...] += brsmall[k % 2]

        @pl.when(m < PAIRS - 2)
        def _():
            pl.semaphore_signal(credit, inc=1, device_id=sibling, device_id_type=MESH)

        @pl.when(m < PAIRS - 1)
        def _():
            astage[k % 2] = acc[...].astype(BF16)
            asmall[k % 2] = accs[...]
            for c in to_owner(k):
                c.start()
        return carry
    lax.fori_loop(0, PAIRS, second, 0)

    def add_in(k, carry):
        for c in to_owner(k):
            c.wait_recv()
        acc[...] += drecv[k - 1].astype(F32)
        accs[...] += srecv[k - 1]
        return carry
    lax.fori_loop(1, PAIRS, add_in, 0)

    rank = acc.shape[0]
    part = rank // 8

    def part_of(i):
        return pl.ds(pl.multiple_of(((seq + i) % 8) * part, part), part)

    def scatter(i):
        return (remote(acc.at[part_of(i)], rs.at[seq], r_ss.at[i - 1], r_rs.at[i - 1], peer(i)),
                remote(accs, rss.at[seq], t_ss.at[i - 1], t_rs.at[i - 1], peer(i)))

    def arrived(i):
        j = (seq + 8 - i) % 8
        return (remote(acc.at[part_of(0)], rs.at[j], r_ss.at[i - 1], r_rs.at[i - 1], peer(i)),
                remote(accs, rss.at[j], t_ss.at[i - 1], t_rs.at[i - 1], peer(i)))

    def gather(i):
        return remote(fin.at[part_of(0)], fin.at[part_of(0)], f_ss.at[i - 1], f_rs.at[i - 1], peer(i))

    def gathered(i):
        return remote(fin.at[part_of(8 - i)], fin.at[part_of(8 - i)], f_ss.at[i - 1], f_rs.at[i - 1], peer(i))

    for i in range(1, PEERS + 1):
        for c in scatter(i):
            c.start()
    rs[seq] = acc[part_of(0), :]
    rss[seq] = accs[...]
    for i in range(1, PEERS + 1):
        for c in arrived(i):
            c.wait_recv()
    total, small = rs[0], rss[0]
    for i in range(1, PEERS + 1):
        total = total + rs[i]
        small = small + rss[i]
    fin[part_of(0), :] = total
    g_small[...] = small
    for i in range(1, PEERS + 1):
        gather(i).start()

    row = lax.broadcasted_iota(jnp.int32, (tokens, blk), 0)
    col = lax.broadcasted_iota(jnp.int32, (tokens, blk), 1)
    on = (row % SUB) == (col // states)
    pick = jnp.where(lax.broadcasted_iota(jnp.int32, (blk, states), 0) % states
                     == lax.broadcasted_iota(jnp.int32, (blk, states), 1), 1.0, 0.0)
    for src, dst in ((oc_s, g_outc), (ic_s, g_inc)):
        x = jnp.where(on, src[SUB:SUB + tokens, :], 0.0)
        dst[...] = jnp.dot(x, pick, preferred_element_type=F32, precision=lax.Precision.HIGHEST)

    for i in range(1, PEERS + 1):
        gathered(i).wait_recv()
    g_w[...] = fin[...]

    send_seg().wait_send()
    for k in range(PAIRS):
        for c in forward_w(k):
            c.wait_send()
        for i in range(1, PEERS + 1):
            send_ends(k, i).wait_send()
    for k in range(1, PAIRS):
        for c in push_w(k):
            c.wait_send()
    for k in (PAIRS - 1, 0):
        for c in to_sibling(k):
            c.wait_send()
    for k in (PAIRS - 2, PAIRS - 1):
        for c in to_owner(k):
            c.wait_send()
    for i in range(1, PEERS + 1):
        for c in scatter(i):
            c.wait_send()
        gather(i).wait_send()


def run(low, w, par, sig, gate, cot, keepb, segb, inb, outb, cmat, bmat, omat):
    tokens, chans = sig.shape
    rank, width = w.shape
    n = outb.shape[0] // tokens
    blk = SUB * n
    nblk = tokens // SUB
    rows16, rows32 = (nblk + 2) * SUB, (nblk + 2) * 2 * SUB
    S = jax.ShapeDtypeStruct
    vm = lambda *shape: pltpu.VMEM(shape, F32)
    vb = lambda *shape: pltpu.VMEM(shape, BF16)
    dma = lambda *shape: pltpu.SemaphoreType.DMA(shape)
    scratch = [
        vb(16, rank, width), vm(16, ROWS, width), vb(rank, tokens), vm(tokens, LANES), vm(SUB, LANES),
        vm(PAIRS, 2, 2 * ROWS, width), vm(PAIRS, PEERS, 2 * ROWS, width),
    ] + [vm(tokens, width)] * 5 + [vm((tokens + 1) * n, width), vm(tokens * n, width)] + [vb(blk, width)] * 8 + [
        vm(rows16, width), vb(rows32, width), vb(rows32, width), vm(rows16, width), vm(rows16, width), vm(rows16, blk), vm(rows16, blk),
        vm(2, rank, width), vm(2, rank, width), vm(2, ROWS, width), vm(2, ROWS, width),
        vb(2, rank, width), vm(2, ROWS, width), vb(PAIRS - 1, rank, width), vm(PAIRS - 1, ROWS, width),
        vm(rank, width), vm(ROWS, width), vm(8, rank // 8, width), vm(8, ROWS, width), vm(rank, width),
    ] + [dma(PAIRS)] * 8 + [dma(PAIRS, PEERS)] * 2 + [dma(PAIRS)] * 8 + [dma(PEERS)] * 6 + [
        pltpu.SemaphoreType.DMA, pltpu.SemaphoreType.DMA, dma(2), pltpu.SemaphoreType.REGULAR]
    points = tokens * n * chans
    return pl.pallas_call(
        kernel,
        in_specs=[pl.BlockSpec(memory_space=pltpu.VMEM)] * 13,
        out_specs=[pl.BlockSpec(memory_space=pltpu.VMEM)] * 7,
        out_shape=[S((tokens, chans), BF16), S((tokens, chans), BF16), S((tokens, rank), F32), S((tokens, n), F32),
                   S((tokens, n), F32), S((rank, width), F32), S((ROWS, width), F32)],
        scratch_shapes=scratch,
        cost_estimate=pl.CostEstimate(flops=30 * points, bytes_accessed=20 << 20, transcendentals=3 * points),
        compiler_params=pltpu.CompilerParams(vmem_limit_bytes=63 << 20, collective_id=0, has_side_effects=True),
        name="scan_backward",
    )(low, w, par, sig, gate, cot, keepb, segb, inb, outb, cmat, bmat, omat)


def tables(coef_in, coef_out):
    n, tokens = coef_in.shape
    nblk = tokens // SUB
    bc = lambda x: jnp.broadcast_to(x.T[:, :, None], (tokens, n, LANES)).reshape(tokens * n, LANES)

    def banded(x):
        xt = x.T
        hi = lax.reduce_precision(xt, 8, 7)
        parts = jnp.stack([hi, xt - hi]).reshape(2, nblk, SUB, 1, n) * jnp.eye(SUB, dtype=F32)[None, None, :, :, None]
        m = parts.transpose(1, 0, 2, 3, 4).reshape(nblk * 2 * SUB, SUB * n)
        return jnp.pad(m, ((2 * SUB, 2 * SUB), (0, 0))).astype(BF16)
    ones = jnp.repeat(jnp.eye(SUB, dtype=F32), n, axis=1).astype(BF16)
    return bc(coef_in), bc(coef_out), banded(coef_out), banded(coef_in), ones


def shards(signal, gating, low_rank, dt_weight, dt_bias, decay_rate, skip_gain, coef_in, coef_out, segment_ids, out_grad):
    n, owned = decay_rate.shape
    par = jnp.concatenate([jnp.maximum(decay_rate, 1e-30), skip_gain[None, :], dt_bias[None, :],
                           jnp.zeros((ROWS - n - 2, owned), F32)], 0)
    seg = segment_ids[0].astype(F32)
    keep = jnp.concatenate([jnp.zeros((1,), F32), (seg[1:] == seg[:-1]).astype(F32)])
    keepb = jnp.broadcast_to(keep[:, None], (keep.shape[0], LANES))
    segb = jnp.broadcast_to(jnp.repeat(jnp.stack([seg[0], seg[-1]]), SUB // 2)[:, None], (SUB, LANES))
    g_sig, g_gate, g_low, g_inc, g_outc, g_w, g_small = run(
        low_rank[0], dt_weight, par, signal[0], gating[0], out_grad[0], keepb, segb, *tables(coef_in[0], coef_out[0]))
    return (g_sig[None], g_gate[None], g_low[None], g_inc.T[None], g_outc.T[None],
            g_w, g_small[:n], g_small[n], g_small[n + 1])


def solution(mesh):
    return jax.shard_map(
        shards,
        mesh=mesh,
        in_specs=(
            P("fsdp", "seq", None), P("fsdp", "seq", None), P("fsdp", "seq", None),
            P(None, "fsdp"), P("fsdp"), P(None, "fsdp"), P("fsdp"),
            P("fsdp", None, "seq"), P("fsdp", None, "seq"), P("fsdp", "seq"), P("fsdp", "seq", None),
        ),
        out_specs=(
            P("fsdp", "seq", None), P("fsdp", "seq", None), P("fsdp", "seq", None),
            P("fsdp", None, "seq"), P("fsdp", None, "seq"), P(None, "fsdp"), P(None, "fsdp"), P("fsdp"), P("fsdp"),
        ),
        check_vma=False,
    )
```

time: 1880 us -> 286 us (0.15); the launches traced: 1850 us -> 285 us
  other arithmetic: 994 us -> 6.36 us
  waiting for transfers between devices: 383 us -> 0 us
  local copies, waits for them, and re-layouts: 286 us -> 23.3 us
  Pallas kernels: 0 us -> 255 us
  blocking collectives: 64.7 us -> 0 us
  starting transfers between devices: 52.5 us -> 0 us
  loops' own time: 28.8 us -> 0 us
  matrix products: 25.3 us -> 0 us
    reduce_sum x75 -> x0, other arithmetic: 383 us -> none  [the longest x64 360 us: full_block(): jnp.sum(adj * (b_blk[offset][:, None] * s_blk[offset][None, :] - rate_all...]
    pallas_call x0 -> x1, Pallas kernels: none -> 255 us  [run(): pl.pallas_call(kernel, in_specs=[pl.BlockSpec(memory_space=pltpu.VMEM)] *...]
    ppermute x15 -> x0, waiting for transfers between devices: 169 us -> none  [from_behind(): return lax.ppermute(x, axis, pairs)]
    mul x40 -> x2, other arithmetic: 162 us -> 0.03 us  [banded(): jnp.stack([hi, xt - hi]).reshape(2, nblk, SUB, 1, n)]
    add x63 -> x0, other arithmetic: 160 us -> none  [the longest x8 96.7 us: forward_block(): decay_of(d_blk[offset], k_blk[offset]) * state]
    reduce_scatter x2 -> x0, waiting for transfers between devices: 149 us -> none  [the longest x1 105 us: shards(): lax.psum_scatter(weight_part, 'fsdp', scatter_dimension=1, tiled=True)]
    sub x9 -> x0, other arithmetic: 138 us -> none  [the longest x8 137 us: full_block(): rate_grad - adj * prior * decays[offset] * d_blk[offset][None, :]]
    neg x121 -> x0, other arithmetic: 128 us -> none  [the longest x120 126 us: decay_of(): return jnp.exp(-d_row[None, :] * rate_all) * k_val]
  transfers between devices with their start and end apart: 19 -> 0, of which waited for: 18 -> 0; matrix products, arithmetic and copies ran while one was open for 2% -> 0% of each run, Pallas kernels for 0% -> 0%
where the time goes in v2:
time: 286 us; the launch traced here: 285 us
  Pallas kernels  255 us (89%)
  local copies, waits for them, and re-layouts  23.3 us (8%)
  other arithmetic  6.36 us (2%)
    pallas_call x1, Pallas kernels, run(): pl.pallas_call(kernel, in_specs=[pl.BlockSpec(memory_space=pltpu.VMEM)] *...  255 us
    unnamed x12, local copies, waits for them, and re-layouts  9.3 us

profile of v2, /device:TPU:4, one launch (start us, length us, event | category | flops | bytes accessed | tf_op | source)
XLA Modules:
  0.0 285.4 jit_solution(5080292572445362791)
XLA Ops:
  0.6 0.7 convert_element_type.31
  1.3 0.1 compare_bitcast_fusion
  1.4 0.1 add_convert_fusion
  1.5 0.1 pad.22.clone
  1.5 0.6 fusion.3
  2.1 1.4 pad_maximum_fusion
  3.5 0.1 broadcast_in_dim.65
  3.6 0.1 broadcast_in_dim.66
  3.6 0.7 broadcast_in_dim.67.segb
  4.3 0.7 bitcast_reduce-precision_fusion
  5.0 0.7 bitcast_reduce-precision_fusion.1
  5.7 0.8 broadcast_maximum_fusion
  6.5 1.4 maximum_maximum_fusion.par_own
  7.9 0.1 stack.22
  8.0 0.1 stack.25
  8.0 0.1 broadcast_in_dim.72
  8.1 0.7 convert_element_type.35.omat
  8.9 0.7 broadcast_in_dim.64.keepb
  9.6 0.1 stack.23
  9.7 0.1 copy.26
  9.8 0.1 stack.26
  9.9 0.1 copy.27
  10.0 0.8 copy.25
  10.8 0.1 broadcast_in_dim.70
  10.9 0.8 copy.24
  11.7 0.1 broadcast_in_dim.68
  11.8 1.3 broadcast_in_dim.69.inb
  13.1 1.3 broadcast_in_dim.71.outb
  14.4 0.6 multiply_convert_fusion
  15.0 1.0 mul.54
  16.0 0.7 pad.10.bmat
  16.7 1.0 mul.49
  17.6 0.7 pad.9.cmat
  18.3 255.0 %scan_backward.1 = (bf16[128,8192]{1,0:T(8,128)(2,1)}, bf16[128,8192]{1,0:T(8,128)(2,1)}, f32[128,512]{1,0:T(8,128)}, f32[128,16]{1,0:T(8,128)}, f32[128,16]{1,0...) custom-call(bf16[128,512]{1,0:T(8,128)(2,1)} %bitcast.65, bf16[512,512]{1,0:T(8,128)(2,1)} %w_own.1, ...), custom_call_target="tpu_custom_call" | custom-call | flops 503316480 | bytes 20971520 | tf_op jit(solution)/shard_map/scan_backward/pallas_call | solution.py:422
  273.3 1.4 fusion.2
  274.7 1.4 slice.35
  276.1 1.5 copy.28
  277.6 1.5 copy.29
  279.1 0.0 copy-start
  279.1 3.2 %copy.34 = bf16[1,128,8192]{2,1,0:T(8,128)(2,1)} copy(bf16[1,128,8192]{2,1,0:T(8,128)(2,1)} %bitcast.52) | data formatting | bytes 4194304
  282.3 0.0 copy-done
  282.3 0.0 copy-start.2
  282.3 0.0 copy-start.1
  282.3 1.3 copy.35
  283.7 0.0 copy-done.2
  283.7 0.7 copy.36
  284.4 0.0 copy-done.1
  284.4 1.0 copy.37
  (5 shorter events, 0.0 us)
Async XLA Ops:
  279.1 3.2 %copy-start = (bf16[128,8192]{1,0:T(8,128)(2,1)S(1)}, bf16[128,8192]{1,0:T(8,128)(2,1)}, u32[]{:S(2)}) copy-start(bf16[128,8192]{1,0:T(8,128)(2,1)} %get-tuple-element.17) | copy-start | bytes 6291460
  282.3 1.3 copy-start.2
  282.3 2.1 copy-start.1

commit v3 on v2

--- a/solution.py
+++ b/solution.py
@@ -28,18 +28,19 @@
     return jnp.maximum(x, 0.0) + jnp.log1p(jnp.exp(-jnp.abs(x)))
 
 
-def kernel(low, w_own, par_own, sig, gate, cot, keepb, segb, inb, outb, cmat, bmat, omat,
-           g_sig, g_gate, g_low, g_inc, g_outc, g_w, g_small,
-           wall, pall, lowt, keep_s, seg_in, xs, er,
-           dk_s, d_s, ds_s, a_s, r_s, hist, dec_s, hb0, hb1, ab0, ab1, al0, al1, zr0, zr1,
-           scan_s, a16, d16, q_s, zz_s, oc_s, ic_s,
+def kernel(low, w_own, rate_own, skip_own, bias_own, sig_hbm, gate_hbm, cot_hbm, seg, c_in, c_out,
+           g_sig, g_gate, g_low, g_inc, g_outc, g_w, g_rate, g_skip, g_bias,
+           sig, gate, cot, par_own, wall, pall, lowt, seg_s, keep_s, inb, outb, ones, xs, er,
+           dk_s, d_s, ds_s, a_s, r_s, hist, dec_s, y0, y1, q0, q1, z0, z1,
+           scan_s, q_s, zz_s, oc_s, ic_s,
            bsend, brecv, bsmall, brsmall, astage, asmall, drecv, srecv, acc, accs, rs, rss, fin,
            w_ss, w_rs, p_ss, p_rs, wf_ss, wf_rs, pf_ss, pf_rs, x_ss, x_rs, b_ss, b_rs, bs_ss, bs_rs,
-           d_ss, d_rs, s_ss, s_rs, r_ss, r_rs, t_ss, t_rs, f_ss, f_rs, seg_ss, seg_rs, own_sem, credit):
+           d_ss, d_rs, s_ss, s_rs, r_ss, r_rs, t_ss, t_rs, f_ss, f_rs, h_ss, h_rs, seg_ss, seg_rs, own_sem, credit):
     tokens = low.shape[0]
     width = w_own.shape[1]
-    states = outb.shape[0] // tokens
-    blk = SUB * states
+    states = rate_own.shape[0]
+    half = states // 2
+    blk = SUB * half
     nblk = tokens // SUB
     seq = lax.axis_index("seq")
     me = lax.axis_index("fsdp")
@@ -47,11 +48,20 @@
     cy, cx = chip // 4, chip % 4
     sibling = (seq, chip * 2 + (1 - core))
 
+    def offset(k):
+        late = k // 6
+        r = k % 3
+        return (1 - late) * (k // 3) + late * (k % 2), (1 - late) * (r + r // 2) + 2 * late
+
+    def device(dy, dx):
+        return (seq, (((cy + dy) % 2) * 4 + (cx + dx) % 4) * 2 + core)
+
     def target(k):
-        return (seq, (((cy + k // 4) % 2) * 4 + (cx + k % 4) % 4) * 2 + core)
+        return device(*offset(k))
 
     def source_chip(k):
-        return ((cy + k // 4) % 2) * 4 + (cx + 4 - k % 4) % 4
+        dy, dx = offset(k)
+        return ((cy + dy) % 2) * 4 + (cx + 4 - dx) % 4
 
     def peer(i):
         return ((seq + i) % 8, me)
@@ -67,34 +77,75 @@
     pl.semaphore_signal(barrier, inc=1, device_id=sibling, device_id_type=MESH)
     pl.semaphore_wait(barrier, PAIRS + PEERS)
 
-    def push_w(k):
-        return (remote(w_own, wall.at[2 * k], w_ss.at[k], w_rs.at[k], target(k)),
-                remote(par_own, pall.at[2 * k], p_ss.at[k], p_rs.at[k], target(k)))
+    def push_p(k):
+        return remote(par_own, pall.at[2 * k], p_ss.at[k], p_rs.at[k], target(k))
+
+    def hop(src, k, dev, part=None):
+        if part is None:
+            return remote(src, wall.at[2 * k], w_ss.at[k], w_rs.at[k], dev)
+        rows = pl.ds(part * (w_own.shape[0] // 2), w_own.shape[0] // 2)
+        return remote(src.at[rows], wall.at[2 * k, rows], h_ss.at[k - 6, part], h_rs.at[k - 6, part], dev)
+
+    right, left, across = device(0, 1), device(0, 3), device(1, 0)
+
+    def hops(k):
+        if k == 1:
+            return [hop(w_own, 1, right)]
+        if k == 2:
+            return [hop(w_own, 2, left)]
+        if k == 3:
+            return [hop(w_own, 3, across)]
+        if k == 4:
+            return [hop(wall.at[6], 4, right)]
+        if k == 5:
+            return [hop(wall.at[6], 5, left)]
+        if k == 6:
+            return [hop(wall.at[2], 6, right, 0), hop(wall.at[4], 6, left, 1)]
+        return [hop(wall.at[12], 7, across, 0), hop(wall.at[12], 7, across, 1)]
 
     def forward_w(k):
         return (remote(wall.at[2 * k], wall.at[2 * k + 1], wf_ss.at[k], wf_rs.at[k], sibling),
                 remote(pall.at[2 * k], pall.at[2 * k + 1], pf_ss.at[k], pf_rs.at[k], sibling))
 
     def send_seg():
-        return remote(segb, seg_in, seg_ss, seg_rs, peer(1))
-
+        return remote(seg_s.at[pl.ds(tokens, 8)], seg_s.at[pl.ds(0, 8)], seg_ss, seg_rs, peer(1))
+
+    inputs = [pltpu.make_async_copy(a, b, own_sem.at[2 + i]) for i, (a, b) in enumerate(((sig_hbm, sig), (gate_hbm, gate), (cot_hbm, cot)))]
+    for k in (1, 2, 3):
+        for c in hops(k):
+            c.start()
+    own = pltpu.make_async_copy(w_own, wall.at[0], own_sem.at[0])
+    own.start()
+    for c in inputs:
+        c.start()
+    par_own[0:states, :] = jnp.maximum(rate_own[...], 1e-30)
+    par_own[states:ROWS, :] = jnp.zeros((ROWS - states, width), F32)
+    par_own[states:states + 1, :] = skip_own[...]
+    par_own[states + 1:states + 2, :] = bias_own[...]
+    for k in range(1, PAIRS):
+        push_p(k).start()
+    ownp = pltpu.make_async_copy(par_own, pall.at[0], own_sem.at[1])
+    ownp.start()
+    seg_s[8:8 + tokens, :] = jnp.broadcast_to(seg[...].astype(F32), (LANES, tokens)).T
     send_seg().start()
-    for k in range(1, 4):
-        for c in push_w(k):
-            c.start()
-    own = (pltpu.make_async_copy(w_own, wall.at[0], own_sem.at[0]), pltpu.make_async_copy(par_own, pall.at[0], own_sem.at[1]))
-    for c in own:
+    own.wait()
+    ownp.wait()
+    for c in forward_w(0):
         c.start()
+    for t in range(tokens):
+        inb[t * states:(t + 1) * states, :] = jnp.broadcast_to(c_in[:, t:t + 1], (states, LANES))
+        outb[t * states:(t + 1) * states, :] = jnp.broadcast_to(c_out[:, t:t + 1], (states, LANES))
+    ones[...] = jnp.where(lax.broadcasted_iota(jnp.int32, (SUB, 2 * blk), 1) % blk // half
+                          == lax.broadcasted_iota(jnp.int32, (SUB, 2 * blk), 0), 1.0, 0.0).astype(BF16)
     lowt[...] = low[...].T
     oc_s[...] = jnp.zeros_like(oc_s)
     ic_s[...] = jnp.zeros_like(ic_s)
     g_low[...] = jnp.zeros_like(g_low)
-    for c in own:
+    send_seg().wait_recv()
+    keep_s[...] = jnp.where(seg_s[8:8 + tokens, :] == seg_s[7:7 + tokens, :], 1.0, 0.0)
+    keep_s[0:1, :] = jnp.where(seq == 0, 0.0, keep_s[0:1, :])
+    for c in inputs:
         c.wait()
-    send_seg().wait_recv()
-    keep_s[...] = keepb[...]
-    same = jnp.where(seg_in[SUB // 2:SUB // 2 + 1, :] == segb[0:1, :], 1.0, 0.0)
-    keep_s[0:1, :] = jnp.where(seq == 0, 0.0, same)
 
     def columns(k, other):
         return pl.ds(pl.multiple_of((source_chip(k) * 2 + (core if other == 0 else 1 - core)) * width, width), width)
@@ -144,18 +195,43 @@
     def send_ends(k, i):
         return remote(xs.at[k, (seq + i) // 8], er.at[k, i - 1], x_ss.at[k, i - 1], x_rs.at[k, i - 1], peer(i))
 
-    def first(k, carry):
-        @pl.when(k > 0)
-        def _():
-            for c in push_w(k):
-                c.wait_recv()
+    def shared(k):
         for c in forward_w(k):
             c.start()
 
-        @pl.when((k > 0) & (k < PAIRS - 3))
-        def _():
-            for c in push_w(k + 3):
+    def came(k):
+        for c in hops(k):
+            c.wait_recv()
+        push_p(k).wait_recv()
+
+    def first(k, carry):
+        @pl.when(k == 1)
+        def _():
+            for j in (1, 2, 3):
+                came(j)
+            for j in (4, 5, 6):
+                for c in hops(j):
+                    c.start()
+            for j in (1, 2, 3):
+                shared(j)
+
+        @pl.when(k == 4)
+        def _():
+            for j in (4, 5):
+                came(j)
+                shared(j)
+
+        @pl.when(k == 5)
+        def _():
+            came(6)
+            for c in hops(7):
                 c.start()
+            shared(6)
+
+        @pl.when(k == 7)
+        def _():
+            came(7)
+            shared(7)
         local_pass(2 * k, columns(k, 0), xs.at[k, 0, pl.ds(0, ROWS)], xs.at[k, 1, pl.ds(0, ROWS)])
         for c in forward_w(k):
             c.wait_recv()
@@ -175,83 +251,88 @@
             ad = jnp.where(seq + i < 8, jnp.exp2(nrate * e[base + states:base + states + 1, :]) * ad + e[base:base + states, :], ad)
         return st, ad
 
-    def split(ref, x):
-        hi = x.astype(BF16)
-        rest = (x - hi.astype(F32)).astype(BF16)
-        for b in range(nblk):
-            ref[2 * SUB * (b + 1):2 * SUB * (b + 1) + SUB, :] = hi[b * SUB:(b + 1) * SUB]
-            ref[2 * SUB * (b + 1) + SUB:2 * SUB * (b + 2), :] = rest[b * SUB:(b + 1) * SUB]
-
-    def both(x):
-        return x[:SUB] + x[SUB:]
+    def folded(x):
+        return x[:half] + x[half:]
+
+    def lane_groups(x):
+        return functools.reduce(lambda p, q: p + q, [x[:, g * LANES:(g + 1) * LANES] for g in range(width // LANES)])
+
+    def ones_dot(x):
+        return jnp.dot(ones[:, 0:x.shape[0]], x, preferred_element_type=F32)
 
     def full_pass(k, slot, cols, base, small):
         raw, delta, ds, a = prepare(slot, cols)
         d_s[...] = delta
         r_s[...] = jax.nn.sigmoid(raw)
-        split(a16, a)
-        split(d16, ds)
         nrate = rates(slot)
         st0, ad0 = entering(k, base, nrate)
         hist[0:states, :] = st0
 
-        def fwd_vec(b, st, hb):
+        def fwd_vec(b, st, y):
+            held = None
             for u in range(SUB):
                 row = pl.multiple_of((b * SUB + u) * states, states)
+                here = pl.ds(row, states)
                 dec = jnp.exp2(nrate * dk_s.at[block(b), :][u:u + 1, :])
-                dec_s[pl.ds(row, states), :] = dec
+                dec_s[here, :] = dec
                 st = dec * st + coef(inb, b * SUB + u) * ds_s.at[block(b), :][u:u + 1, :]
                 hist[pl.ds(row + states, states), :] = st
-                hb[u * states:(u + 1) * states, :] = st.astype(BF16)
+                oc_s[here, :] += lane_groups(st * a_s.at[block(b), :][u:u + 1, :])
+                part = folded(st * coef(outb, b * SUB + u))
+                if u % 2:
+                    y[(u - 1) * half:(u + 1) * half, :] = jnp.concatenate([held, part], 0).astype(BF16)
+                held = part
             return st
 
-        def rows(b, size):
-            return pl.ds(pl.multiple_of((b + 1) * size, size), size)
-
-        def fwd_mat(b, hb):
-            h = hb[...]
-            scan_s[rows(b, SUB), :] = both(jnp.dot(cmat[rows(b, 2 * SUB), :], h, preferred_element_type=F32))
-            oc_s[rows(b, SUB), :] += both(nt(a16[rows(b, 2 * SUB), :], h))
+        def rows(b):
+            return pl.ds(pl.multiple_of((b + 1) * SUB, SUB), SUB)
+
+        def fwd_mat(b, y):
+            scan_s[rows(b), :] = ones_dot(y[...])
 
         def fwd(i, st):
-            st = fwd_vec(2 * i, st, hb0)
-            fwd_mat(2 * i - 1, hb1)
-            st = fwd_vec(2 * i + 1, st, hb1)
-            fwd_mat(2 * i, hb0)
+            st = fwd_vec(2 * i, st, y0)
+            fwd_mat(2 * i - 1, y1)
+            st = fwd_vec(2 * i + 1, st, y1)
+            fwd_mat(2 * i, y0)
             return st
         lax.fori_loop(0, nblk // 2, fwd, st0)
-        fwd_mat(nblk - 1, hb1)
-
-        def bwd_vec(b, ca, rg, ab, al, zr):
+        fwd_mat(nblk - 1, y1)
+
+        def bwd_vec(b, ca, rg, qb, zb):
+            held = None
             for u in reversed(range(SUB)):
                 row = pl.multiple_of((b * SUB + u) * states, states)
+                here = pl.ds(row, states)
                 adj = coef(outb, b * SUB + u) * a_s.at[block(b), :][u:u + 1, :] + ca
-                hi = adj.astype(BF16)
-                ab[u * states:(u + 1) * states, :] = hi
-                al[u * states:(u + 1) * states, :] = (adj - hi.astype(F32)).astype(BF16)
-                ca = dec_s[pl.ds(row, states), :] * adj
-                z = ca * hist[pl.ds(row, states), :]
-                zr[u * states:(u + 1) * states, :] = (z * nrate).astype(BF16)
+                ic_s[here, :] += lane_groups(adj * ds_s.at[block(b), :][u:u + 1, :])
+                ca = dec_s[here, :] * adj
+                z = ca * hist[here, :]
                 rg = rg + z * d_s.at[block(b), :][u:u + 1, :]
+                part = folded(adj * coef(inb, b * SUB + u)), folded(z * nrate)
+                if u % 2 == 0:
+                    at = slice(u * half, (u + 2) * half)
+                    pair = jnp.concatenate([part[0], held[0]], 0)
+                    hi = pair.astype(BF16)
+                    qb[at, :] = hi
+                    qb[blk + u * half:blk + (u + 2) * half, :] = (pair - hi.astype(F32)).astype(BF16)
+                    zb[at, :] = jnp.concatenate([part[1], held[1]], 0).astype(BF16)
+                held = part
             return ca, rg
 
-        def bwd_mat(b, ab, al, zr):
-            h = ab[...]
-            bm = bmat[rows(b, 2 * SUB), :]
-            q_s[rows(b, SUB), :] = (both(jnp.dot(bm, h, preferred_element_type=F32))
-                                    + jnp.dot(bm[:SUB], al[...], preferred_element_type=F32))
-            zz_s[rows(b, SUB), :] = jnp.dot(omat[...], zr[...], preferred_element_type=F32)
-            ic_s[rows(b, SUB), :] += both(nt(d16[rows(b, 2 * SUB), :], h))
+        def bwd_mat(b, qb, zb):
+            q_s[rows(b), :] = ones_dot(qb[...])
+            zz_s[rows(b), :] = ones_dot(zb[...])
 
         def bwd(i, carry):
             b = nblk - 1 - 2 * i
-            carry = bwd_vec(b, *carry, ab0, al0, zr0)
-            bwd_mat(b + 1, ab1, al1, zr1)
-            carry = bwd_vec(b - 1, *carry, ab1, al1, zr1)
-            bwd_mat(b, ab0, al0, zr0)
+            carry = bwd_vec(b, *carry, q0, z0)
+            bwd_mat(b + 1, q1, z1)
+            carry = bwd_vec(b - 1, *carry, q1, z1)
+            bwd_mat(b, q0, z0)
             return carry
         _, rg = lax.fori_loop(0, nblk // 2, bwd, (ad0, jnp.zeros((states, width), F32)))
-        bwd_mat(0, ab1, al1, zr1)
+        bwd_mat(0, q1, z1)
 
         q = q_s[SUB:SUB + tokens, :]
         s = sig[:, cols].astype(F32)
@@ -359,18 +440,15 @@
         total = total + rs[i]
         small = small + rss[i]
     fin[part_of(0), :] = total
-    g_small[...] = small
+    g_rate[...] = small[0:states]
+    g_skip[...] = small[states:states + 1]
+    g_bias[...] = small[states + 1:states + 2]
     for i in range(1, PEERS + 1):
         gather(i).start()
 
-    row = lax.broadcasted_iota(jnp.int32, (tokens, blk), 0)
-    col = lax.broadcasted_iota(jnp.int32, (tokens, blk), 1)
-    on = (row % SUB) == (col // states)
-    pick = jnp.where(lax.broadcasted_iota(jnp.int32, (blk, states), 0) % states
-                     == lax.broadcasted_iota(jnp.int32, (blk, states), 1), 1.0, 0.0)
     for src, dst in ((oc_s, g_outc), (ic_s, g_inc)):
-        x = jnp.where(on, src[SUB:SUB + tokens, :], 0.0)
-        dst[...] = jnp.dot(x, pick, preferred_element_type=F32, precision=lax.Precision.HIGHEST)
+        for n in range(states):
+            dst[n:n + 1, :] = jnp.sum(src[pl.ds(n, tokens, stride=states), :].T, 0, keepdims=True)
 
     for i in range(1, PEERS + 1):
         gathered(i).wait_recv()
@@ -383,8 +461,9 @@
         for i in range(1, PEERS + 1):
             send_ends(k, i).wait_send()
     for k in range(1, PAIRS):
-        for c in push_w(k):
+        for c in hops(k):
             c.wait_send()
+        push_p(k).wait_send()
     for k in (PAIRS - 1, 0):
         for c in to_sibling(k):
             c.wait_send()
@@ -397,68 +476,48 @@
         gather(i).wait_send()
 
 
-def run(low, w, par, sig, gate, cot, keepb, segb, inb, outb, cmat, bmat, omat):
+def run(low, w, rate, skip, bias, sig, gate, cot, seg, c_in, c_out):
     tokens, chans = sig.shape
     rank, width = w.shape
-    n = outb.shape[0] // tokens
-    blk = SUB * n
-    nblk = tokens // SUB
-    rows16, rows32 = (nblk + 2) * SUB, (nblk + 2) * 2 * SUB
+    n = rate.shape[0]
+    blk = SUB * n // 2
+    rows16 = (tokens // SUB + 2) * SUB
     S = jax.ShapeDtypeStruct
     vm = lambda *shape: pltpu.VMEM(shape, F32)
     vb = lambda *shape: pltpu.VMEM(shape, BF16)
     dma = lambda *shape: pltpu.SemaphoreType.DMA(shape)
-    scratch = [
-        vb(16, rank, width), vm(16, ROWS, width), vb(rank, tokens), vm(tokens, LANES), vm(SUB, LANES),
+    scratch = [vb(tokens, chans)] * 3 + [
+        vm(ROWS, width), vb(16, rank, width), vm(16, ROWS, width), vb(rank, tokens), vm(tokens + 8, LANES), vm(tokens, LANES),
+        vm(tokens * n, LANES), vm(tokens * n, LANES), vb(SUB, 2 * blk),
         vm(PAIRS, 2, 2 * ROWS, width), vm(PAIRS, PEERS, 2 * ROWS, width),
-    ] + [vm(tokens, width)] * 5 + [vm((tokens + 1) * n, width), vm(tokens * n, width)] + [vb(blk, width)] * 8 + [
-        vm(rows16, width), vb(rows32, width), vb(rows32, width), vm(rows16, width), vm(rows16, width), vm(rows16, blk), vm(rows16, blk),
+    ] + [vm(tokens, width)] * 5 + [vm((tokens + 1) * n, width), vm(tokens * n, width)] + [
+        vb(blk, width), vb(blk, width), vb(2 * blk, width), vb(2 * blk, width), vb(blk, width), vb(blk, width),
+        vm(rows16, width), vm(rows16, width), vm(rows16, width), vm(tokens * n, LANES), vm(tokens * n, LANES),
         vm(2, rank, width), vm(2, rank, width), vm(2, ROWS, width), vm(2, ROWS, width),
         vb(2, rank, width), vm(2, ROWS, width), vb(PAIRS - 1, rank, width), vm(PAIRS - 1, ROWS, width),
         vm(rank, width), vm(ROWS, width), vm(8, rank // 8, width), vm(8, ROWS, width), vm(rank, width),
-    ] + [dma(PAIRS)] * 8 + [dma(PAIRS, PEERS)] * 2 + [dma(PAIRS)] * 8 + [dma(PEERS)] * 6 + [
-        pltpu.SemaphoreType.DMA, pltpu.SemaphoreType.DMA, dma(2), pltpu.SemaphoreType.REGULAR]
+    ] + [dma(PAIRS)] * 8 + [dma(PAIRS, PEERS)] * 2 + [dma(PAIRS)] * 8 + [dma(PEERS)] * 6 + [dma(2, 2)] * 2 + [
+        pltpu.SemaphoreType.DMA, pltpu.SemaphoreType.DMA, dma(5), pltpu.SemaphoreType.REGULAR]
     points = tokens * n * chans
+    vmem, hbm = pl.BlockSpec(memory_space=pltpu.VMEM), pl.BlockSpec(memory_space=pl.ANY)
     return pl.pallas_call(
         kernel,
-        in_specs=[pl.BlockSpec(memory_space=pltpu.VMEM)] * 13,
-        out_specs=[pl.BlockSpec(memory_space=pltpu.VMEM)] * 7,
-        out_shape=[S((tokens, chans), BF16), S((tokens, chans), BF16), S((tokens, rank), F32), S((tokens, n), F32),
-                   S((tokens, n), F32), S((rank, width), F32), S((ROWS, width), F32)],
+        in_specs=[vmem] * 5 + [hbm] * 3 + [vmem] * 3,
+        out_specs=[vmem] * 9,
+        out_shape=[S((tokens, chans), BF16), S((tokens, chans), BF16), S((tokens, rank), F32), S((n, tokens), F32),
+                   S((n, tokens), F32), S((rank, width), F32), S((n, width), F32), S((1, width), F32), S((1, width), F32)],
         scratch_shapes=scratch,
         cost_estimate=pl.CostEstimate(flops=30 * points, bytes_accessed=20 << 20, transcendentals=3 * points),
         compiler_params=pltpu.CompilerParams(vmem_limit_bytes=63 << 20, collective_id=0, has_side_effects=True),
         name="scan_backward",
-    )(low, w, par, sig, gate, cot, keepb, segb, inb, outb, cmat, bmat, omat)
-
-
-def tables(coef_in, coef_out):
-    n, tokens = coef_in.shape
-    nblk = tokens // SUB
-    bc = lambda x: jnp.broadcast_to(x.T[:, :, None], (tokens, n, LANES)).reshape(tokens * n, LANES)
-
-    def banded(x):
-        xt = x.T
-        hi = lax.reduce_precision(xt, 8, 7)
-        parts = jnp.stack([hi, xt - hi]).reshape(2, nblk, SUB, 1, n) * jnp.eye(SUB, dtype=F32)[None, None, :, :, None]
-        m = parts.transpose(1, 0, 2, 3, 4).reshape(nblk * 2 * SUB, SUB * n)
-        return jnp.pad(m, ((2 * SUB, 2 * SUB), (0, 0))).astype(BF16)
-    ones = jnp.repeat(jnp.eye(SUB, dtype=F32), n, axis=1).astype(BF16)
-    return bc(coef_in), bc(coef_out), banded(coef_out), banded(coef_in), ones
+    )(low, w, rate, skip, bias, sig, gate, cot, seg, c_in, c_out)
 
 
 def shards(signal, gating, low_rank, dt_weight, dt_bias, decay_rate, skip_gain, coef_in, coef_out, segment_ids, out_grad):
-    n, owned = decay_rate.shape
-    par = jnp.concatenate([jnp.maximum(decay_rate, 1e-30), skip_gain[None, :], dt_bias[None, :],
-                           jnp.zeros((ROWS - n - 2, owned), F32)], 0)
-    seg = segment_ids[0].astype(F32)
-    keep = jnp.concatenate([jnp.zeros((1,), F32), (seg[1:] == seg[:-1]).astype(F32)])
-    keepb = jnp.broadcast_to(keep[:, None], (keep.shape[0], LANES))
-    segb = jnp.broadcast_to(jnp.repeat(jnp.stack([seg[0], seg[-1]]), SUB // 2)[:, None], (SUB, LANES))
-    g_sig, g_gate, g_low, g_inc, g_outc, g_w, g_small = run(
-        low_rank[0], dt_weight, par, signal[0], gating[0], out_grad[0], keepb, segb, *tables(coef_in[0], coef_out[0]))
-    return (g_sig[None], g_gate[None], g_low[None], g_inc.T[None], g_outc.T[None],
-            g_w, g_small[:n], g_small[n], g_small[n + 1])
+    g_sig, g_gate, g_low, g_inc, g_outc, g_w, g_rate, g_skip, g_bias = run(
+        low_rank[0], dt_weight, decay_rate, skip_gain[None], dt_bias[None], signal[0], gating[0], out_grad[0],
+        segment_ids, coef_in[0], coef_out[0])
+    return (g_sig[None], g_gate[None], g_low[None], g_inc[None], g_outc[None], g_w, g_rate, g_skip[0], g_bias[0])
 
 
 def solution(mesh):

time: 286 us -> 238 us (0.83)
  Pallas kernels: 255 us -> 226 us
  local copies, waits for them, and re-layouts: 23.3 us -> 9.24 us
  other arithmetic: 6.36 us -> 0 us
    pallas_call x1, Pallas kernels: 255 us -> 226 us  [run(): pl.pallas_call(kernel, in_specs=[vmem] * 5 + [hbm] * 3 + [vmem] * 3, out_...]
    broadcast_in_dim x10 -> x0, local copies, waits for them, and re-layouts: 4.41 us -> none  [the longest x4 2.78 us: tables(): jnp.broadcast_to(x.T[:, :, None], (tokens, n, LANES))]
    slice x3 -> x0, local copies, waits for them, and re-layouts: 3.34 us -> none  [the longest x1 1.38 us: shards(): g_small[n + 1]]
    unnamed x12 -> x25, local copies, waits for them, and re-layouts: 9.3 us -> 9.24 us
where the time goes in v3:
time: 238 us; the launch traced here: 236 us
  Pallas kernels  226 us (95%)
  local copies, waits for them, and re-layouts  9.24 us (4%)
    pallas_call x1, Pallas kernels, run(): pl.pallas_call(kernel, in_specs=[vmem] * 5 + [hbm] * 3 + [vmem] * 3, out_...  226 us
    unnamed x25, local copies, waits for them, and re-layouts  9.24 us

profile of v3, /device:TPU:4, one launch (start us, length us, event | category | flops | bytes accessed | tf_op | source)
XLA Modules:
  0.0 235.5 jit_solution(16846912732869884725)
XLA Ops:
  0.6 225.6 %scan_backward.1 = (bf16[128,8192]{1,0:T(8,128)(2,1)}, bf16[128,8192]{1,0:T(8,128)(2,1)}, f32[128,512]{1,0:T(8,128)}, f32[16,128]{1,0:T(8,128)}, f32[16,128]{1,0...) custom-call(bf16[128,512]{1,0:T(8,128)(2,1)} %bitcast.25, ...), custom_call_target="tpu_custom_call" | custom-call | flops 503316480 | bytes 20971520 | tf_op jit(solution)/shard_map/scan_backward/pallas_call | solution.py:503
  226.3 0.0 copy-start
  226.3 3.2 %copy.29 = bf16[1,128,8192]{2,1,0:T(8,128)(2,1)} copy(bf16[1,128,8192]{2,1,0:T(8,128)(2,1)} %bitcast.16) | data formatting | bytes 4194304
  229.5 0.0 copy-done
  229.5 0.0 copy-start.2
  229.5 0.0 copy-start.5
  229.5 0.0 copy-start.4
  229.5 0.0 copy-start.1
  229.5 1.3 copy.30
  230.9 0.0 copy-done.2
  230.9 0.0 copy-start.3
  230.9 0.0 copy-start.7
  230.9 0.0 copy-start.6
  230.9 0.7 copy.31
  231.6 0.0 copy-done.5
  231.6 0.6 copy.32
  232.2 0.0 copy-done.4
  232.2 0.6 copy.33
  232.8 0.0 copy-done.1
  232.8 1.0 copy.34
  233.8 0.0 copy-done.3
  233.8 0.6 copy.35
  234.4 0.0 copy-done.7
  234.4 0.6 copy.36
  235.0 0.0 copy-done.6
  235.0 0.6 copy.37
Async XLA Ops:
  226.3 3.3 %copy-start = (bf16[128,8192]{1,0:T(8,128)(2,1)S(1)}, bf16[128,8192]{1,0:T(8,128)(2,1)}, u32[]{:S(2)}) copy-start(bf16[128,8192]{1,0:T(8,128)(2,1)} %get-tuple-element.19) | copy-start | bytes 6291460
  229.5 1.3 copy-start.2
  229.5 2.1 copy-start.5
  229.5 2.7 %copy-start.4 = (f32[16,128]{1,0:T(8,128)S(1)}, f32[16,128]{1,0:T(8,128)}, u32[]{:S(2)}) copy-start(f32[16,128]{1,0:T(8,128)} %get-tuple-element.22) | copy-start | bytes 24580
  229.5 3.3 %copy-start.1 = (f32[512,512]{1,0:T(8,128)S(1)}, f32[512,512]{1,0:T(8,128)}, u32[]{:S(2)}) copy-start(f32[512,512]{1,0:T(8,128)} %get-tuple-element.41) | copy-start | bytes 3145732
  230.9 2.9 %copy-start.3 = (f32[16,512]{1,0:T(8,128)S(1)}, f32[16,512]{1,0:T(8,128)}, u32[]{:S(2)}) copy-start(f32[16,512]{1,0:T(8,128)} %get-tuple-element.42) | copy-start | bytes 98308
  230.9 3.5 %copy-start.7 = (f32[1,512]{1,0:T(1,128)S(1)}, f32[1,512]{1,0:T(1,128)}, u32[]{:S(2)}) copy-start(f32[1,512]{1,0:T(1,128)} %get-tuple-element.25) | copy-start | bytes 6148
  230.9 4.1 %copy-start.6 = (f32[1,512]{1,0:T(1,128)S(1)}, f32[1,512]{1,0:T(1,128)}, u32[]{:S(2)}) copy-start(f32[1,512]{1,0:T(1,128)} %get-tuple-element.26) | copy-start | bytes 6148

commit v4 on v3

--- a/solution.py
+++ b/solution.py
@@ -13,6 +13,7 @@
 PEERS = 7
 PAIRS = 8
 ROWS = 24
+ENDS = 40
 MESH = pl.DeviceIdType.MESH
 
 
@@ -30,10 +31,10 @@
 
 def kernel(low, w_own, rate_own, skip_own, bias_own, sig_hbm, gate_hbm, cot_hbm, seg, c_in, c_out,
            g_sig, g_gate, g_low, g_inc, g_outc, g_w, g_rate, g_skip, g_bias,
-           sig, gate, cot, par_own, wall, pall, lowt, seg_s, keep_s, inb, outb, ones, xs, er,
+           sig, gate, cot, par_own, wall, pall, lowt, seg_s, keep_s, inb, outb, ones, ones32, xs, er,
            dk_s, d_s, ds_s, a_s, r_s, hist, dec_s, y0, y1, q0, q1, z0, z1,
            scan_s, q_s, zz_s, oc_s, ic_s,
-           bsend, brecv, bsmall, brsmall, astage, asmall, drecv, srecv, acc, accs, rs, rss, fin,
+           bsend, brecv, bsmall, brsmall, astage, asmall, drecv, srecv, acc, accs, accb, rs, rss, fin,
            w_ss, w_rs, p_ss, p_rs, wf_ss, wf_rs, pf_ss, pf_rs, x_ss, x_rs, b_ss, b_rs, bs_ss, bs_rs,
            d_ss, d_rs, s_ss, s_rs, r_ss, r_rs, t_ss, t_rs, f_ss, f_rs, h_ss, h_rs, seg_ss, seg_rs, own_sem, credit):
     tokens = low.shape[0]
@@ -101,7 +102,7 @@
             return [hop(wall.at[6], 5, left)]
         if k == 6:
             return [hop(wall.at[2], 6, right, 0), hop(wall.at[4], 6, left, 1)]
-        return [hop(wall.at[12], 7, across, 0), hop(wall.at[12], 7, across, 1)]
+        return [hop(wall.at[8], 7, right, 0), hop(wall.at[10], 7, left, 1)]
 
     def forward_w(k):
         return (remote(wall.at[2 * k], wall.at[2 * k + 1], wf_ss.at[k], wf_rs.at[k], sibling),
@@ -137,6 +138,8 @@
         outb[t * states:(t + 1) * states, :] = jnp.broadcast_to(c_out[:, t:t + 1], (states, LANES))
     ones[...] = jnp.where(lax.broadcasted_iota(jnp.int32, (SUB, 2 * blk), 1) % blk // half
                           == lax.broadcasted_iota(jnp.int32, (SUB, 2 * blk), 0), 1.0, 0.0).astype(BF16)
+    ones32[...] = jnp.where(lax.broadcasted_iota(jnp.int32, (2 * SUB, 2 * blk), 1) // half
+                            == lax.broadcasted_iota(jnp.int32, (2 * SUB, 2 * blk), 0), 1.0, 0.0).astype(BF16)
     lowt[...] = low[...].T
     oc_s[...] = jnp.zeros_like(oc_s)
     ic_s[...] = jnp.zeros_like(ic_s)
@@ -170,7 +173,7 @@
     def coef(ref, t):
         return wide(ref[pl.ds(pl.multiple_of(t * states, states), states), :], width)
 
-    def local_pass(slot, cols, up, down):
+    def local_pass(slot, cols, up, down, second):
         prepare(slot, cols)
         nrate = rates(slot)
 
@@ -186,11 +189,14 @@
             return st, ad
         zero = jnp.zeros((states, width), F32)
         st, ad = lax.fori_loop(0, nblk, body, (zero, zero))
-        total = jnp.broadcast_to(jnp.sum(dk_s[...], 0, keepdims=True), (ROWS - states, width))
-        up[0:states, :] = st
-        up[states:ROWS, :] = total
-        down[0:states, :] = ad
-        down[states:ROWS, :] = total
+        total = jnp.sum(dk_s[...], 0, keepdims=True)
+        at = pl.ds(second * states, states)
+        last = ENDS - 2 * states if not second else 1
+        total = jnp.broadcast_to(total, (last, width))
+        up[at, :] = st
+        down[at, :] = ad
+        up[2 * states + second:2 * states + second + last, :] = total
+        down[2 * states + second:2 * states + second + last, :] = total
 
     def send_ends(k, i):
         return remote(xs.at[k, (seq + i) // 8], er.at[k, i - 1], x_ss.at[k, i - 1], x_rs.at[k, i - 1], peer(i))
@@ -219,36 +225,38 @@
         def _():
             for j in (4, 5):
                 came(j)
-                shared(j)
-
-        @pl.when(k == 5)
-        def _():
-            came(6)
             for c in hops(7):
                 c.start()
+            for j in (4, 5):
+                shared(j)
+
+        @pl.when(k == 6)
+        def _():
+            came(6)
             shared(6)
 
         @pl.when(k == 7)
         def _():
             came(7)
             shared(7)
-        local_pass(2 * k, columns(k, 0), xs.at[k, 0, pl.ds(0, ROWS)], xs.at[k, 1, pl.ds(0, ROWS)])
+        local_pass(2 * k, columns(k, 0), xs.at[k, 0], xs.at[k, 1], 0)
         for c in forward_w(k):
             c.wait_recv()
-        local_pass(2 * k + 1, columns(k, 1), xs.at[k, 0, pl.ds(ROWS, ROWS)], xs.at[k, 1, pl.ds(ROWS, ROWS)])
+        local_pass(2 * k + 1, columns(k, 1), xs.at[k, 0], xs.at[k, 1], 1)
         for i in range(1, PEERS + 1):
             send_ends(k, i).start()
         return carry
     lax.fori_loop(0, PAIRS, first, 0)
 
     def entering(k, base, nrate):
+        total = 2 * states + base // states
         st = jnp.zeros((states, width), F32)
         ad = jnp.zeros((states, width), F32)
         for i in range(PEERS, 0, -1):
             e = er.at[k, i - 1]
-            st = jnp.where(seq >= i, jnp.exp2(nrate * e[base + states:base + states + 1, :]) * st + e[base:base + states, :], st)
+            st = jnp.where(seq >= i, jnp.exp2(nrate * e[total:total + 1, :]) * st + e[base:base + states, :], st)
             e = er.at[k, PEERS - i]
-            ad = jnp.where(seq + i < 8, jnp.exp2(nrate * e[base + states:base + states + 1, :]) * ad + e[base:base + states, :], ad)
+            ad = jnp.where(seq + i < 8, jnp.exp2(nrate * e[total:total + 1, :]) * ad + e[base:base + states, :], ad)
         return st, ad
 
     def folded(x):
@@ -257,8 +265,8 @@
     def lane_groups(x):
         return functools.reduce(lambda p, q: p + q, [x[:, g * LANES:(g + 1) * LANES] for g in range(width // LANES)])
 
-    def ones_dot(x):
-        return jnp.dot(ones[:, 0:x.shape[0]], x, preferred_element_type=F32)
+    def ones_dot(m, x):
+        return jnp.dot(m[...], x[...], preferred_element_type=F32)
 
     def full_pass(k, slot, cols, base, small):
         raw, delta, ds, a = prepare(slot, cols)
@@ -268,7 +276,7 @@
         st0, ad0 = entering(k, base, nrate)
         hist[0:states, :] = st0
 
-        def fwd_vec(b, st, y):
+        def fwd_vec(b, st, y, off):
             held = None
             for u in range(SUB):
                 row = pl.multiple_of((b * SUB + u) * states, states)
@@ -280,26 +288,27 @@
                 oc_s[here, :] += lane_groups(st * a_s.at[block(b), :][u:u + 1, :])
                 part = folded(st * coef(outb, b * SUB + u))
                 if u % 2:
-                    y[(u - 1) * half:(u + 1) * half, :] = jnp.concatenate([held, part], 0).astype(BF16)
+                    y[off + (u - 1) * half:off + (u + 1) * half, :] = jnp.concatenate([held, part], 0).astype(BF16)
                 held = part
             return st
 
-        def rows(b):
-            return pl.ds(pl.multiple_of((b + 1) * SUB, SUB), SUB)
+        def rows(b, size):
+            return pl.ds(pl.multiple_of((b + 1) * size, size), size)
 
         def fwd_mat(b, y):
-            scan_s[rows(b), :] = ones_dot(y[...])
+            scan_s[rows(b, 2 * SUB), :] = ones_dot(ones32, y)
 
         def fwd(i, st):
-            st = fwd_vec(2 * i, st, y0)
+            st = fwd_vec(4 * i, st, y0, 0)
             fwd_mat(2 * i - 1, y1)
-            st = fwd_vec(2 * i + 1, st, y1)
+            st = fwd_vec(4 * i + 1, st, y0, blk)
+            st = fwd_vec(4 * i + 2, st, y1, 0)
             fwd_mat(2 * i, y0)
-            return st
-        lax.fori_loop(0, nblk // 2, fwd, st0)
-        fwd_mat(nblk - 1, y1)
-
-        def bwd_vec(b, ca, rg, qb, zb):
+            return fwd_vec(4 * i + 3, st, y1, blk)
+        lax.fori_loop(0, nblk // 4, fwd, st0)
+        fwd_mat(nblk // 2 - 1, y1)
+
+        def bwd_vec(b, ca, rg, qb, zb, off):
             held = None
             for u in reversed(range(SUB)):
                 row = pl.multiple_of((b * SUB + u) * states, states)
@@ -316,23 +325,33 @@
                     hi = pair.astype(BF16)
                     qb[at, :] = hi
                     qb[blk + u * half:blk + (u + 2) * half, :] = (pair - hi.astype(F32)).astype(BF16)
-                    zb[at, :] = jnp.concatenate([part[1], held[1]], 0).astype(BF16)
+                    zb[off + u * half:off + (u + 2) * half, :] = jnp.concatenate([part[1], held[1]], 0).astype(BF16)
                 held = part
             return ca, rg
 
-        def bwd_mat(b, qb, zb):
-            q_s[rows(b), :] = ones_dot(qb[...])
-            zz_s[rows(b), :] = ones_dot(zb[...])
+        def q_mat(b, qb):
+            q_s[rows(b, SUB), :] = ones_dot(ones, qb)
+
+        def z_mat(b, zb):
+            zz_s[rows(b, 2 * SUB), :] = ones_dot(ones32, zb)
 
         def bwd(i, carry):
-            b = nblk - 1 - 2 * i
-            carry = bwd_vec(b, *carry, q0, z0)
-            bwd_mat(b + 1, q1, z1)
-            carry = bwd_vec(b - 1, *carry, q1, z1)
-            bwd_mat(b, q0, z0)
+            b = nblk - 1 - 4 * i
+            g = nblk // 2 - 1 - 2 * i
+            carry = bwd_vec(b, *carry, q0, z0, blk)
+            q_mat(b + 1, q1)
+            z_mat(g + 1, z1)
+            carry = bwd_vec(b - 1, *carry, q1, z0, 0)
+            q_mat(b, q0)
+            carry = bwd_vec(b - 2, *carry, q0, z1, blk)
+            q_mat(b - 1, q1)
+            z_mat(g, z0)
+            carry = bwd_vec(b - 3, *carry, q1, z1, 0)
+            q_mat(b - 2, q0)
             return carry
-        _, rg = lax.fori_loop(0, nblk // 2, bwd, (ad0, jnp.zeros((states, width), F32)))
-        bwd_mat(0, q1, z1)
+        _, rg = lax.fori_loop(0, nblk // 4, bwd, (ad0, jnp.zeros((states, width), F32)))
+        q_mat(0, q1)
+        z_mat(0, z1)
 
         q = q_s[SUB:SUB + tokens, :]
         s = sig[:, cols].astype(F32)
@@ -341,9 +360,9 @@
         sg = jax.nn.sigmoid(g)
         av = a_s[...]
         gain = pall[slot, states:states + 1, :]
-        g_gate[:, cols] = (o * (scan_s[SUB:SUB + tokens, :] + gain * s) * sg * (1.0 + g * (1.0 - sg))).astype(BF16)
+        g_gate[:, cols] = (o * (scan_s[2 * SUB:2 * SUB + tokens, :] + gain * s) * sg * (1.0 + g * (1.0 - sg))).astype(BF16)
         g_sig[:, cols] = (d_s[...] * q + gain * av).astype(BF16)
-        rawg = (s * q + zz_s[SUB:SUB + tokens, :] * (1.0 / LOG2E)) * r_s[...]
+        rawg = (s * q + zz_s[2 * SUB:2 * SUB + tokens, :] * (1.0 / LOG2E)) * r_s[...]
         small[0:states, :] = -rg
         small[states:ROWS, :] = jnp.zeros((ROWS - states, width), F32)
         small[states:states + 1, :] = jnp.sum(s * av, 0, keepdims=True)
@@ -371,7 +390,7 @@
             for c in to_sibling(m - 1):
                 c.wait_send()
             pl.semaphore_wait(credit, 1)
-        bsend[k % 2] = full_pass(k, 2 * k + 1, columns(k, 1), ROWS, bsmall.at[k % 2])
+        bsend[k % 2] = full_pass(k, 2 * k + 1, columns(k, 1), states, bsmall.at[k % 2])
         for c in to_sibling(k):
             c.start()
 
@@ -413,12 +432,12 @@
         return pl.ds(pl.multiple_of(((seq + i) % 8) * part, part), part)
 
     def scatter(i):
-        return (remote(acc.at[part_of(i)], rs.at[seq], r_ss.at[i - 1], r_rs.at[i - 1], peer(i)),
+        return (remote(accb.at[part_of(i)], rs.at[seq], r_ss.at[i - 1], r_rs.at[i - 1], peer(i)),
                 remote(accs, rss.at[seq], t_ss.at[i - 1], t_rs.at[i - 1], peer(i)))
 
     def arrived(i):
         j = (seq + 8 - i) % 8
-        return (remote(acc.at[part_of(0)], rs.at[j], r_ss.at[i - 1], r_rs.at[i - 1], peer(i)),
+        return (remote(accb.at[part_of(0)], rs.at[j], r_ss.at[i - 1], r_rs.at[i - 1], peer(i)),
                 remote(accs, rss.at[j], t_ss.at[i - 1], t_rs.at[i - 1], peer(i)))
 
     def gather(i):
@@ -427,17 +446,18 @@
     def gathered(i):
         return remote(fin.at[part_of(8 - i)], fin.at[part_of(8 - i)], f_ss.at[i - 1], f_rs.at[i - 1], peer(i))
 
+    accb[...] = acc[...].astype(BF16)
     for i in range(1, PEERS + 1):
         for c in scatter(i):
             c.start()
-    rs[seq] = acc[part_of(0), :]
+    rs[seq] = accb[part_of(0), :]
     rss[seq] = accs[...]
     for i in range(1, PEERS + 1):
         for c in arrived(i):
             c.wait_recv()
-    total, small = rs[0], rss[0]
-    for i in range(1, PEERS + 1):
-        total = total + rs[i]
+    total, small = rs[0].astype(F32), rss[0]
+    for i in range(1, PEERS + 1):
+        total = total + rs[i].astype(F32)
         small = small + rss[i]
     fin[part_of(0), :] = total
     g_rate[...] = small[0:states]
@@ -488,14 +508,14 @@
     dma = lambda *shape: pltpu.SemaphoreType.DMA(shape)
     scratch = [vb(tokens, chans)] * 3 + [
         vm(ROWS, width), vb(16, rank, width), vm(16, ROWS, width), vb(rank, tokens), vm(tokens + 8, LANES), vm(tokens, LANES),
-        vm(tokens * n, LANES), vm(tokens * n, LANES), vb(SUB, 2 * blk),
-        vm(PAIRS, 2, 2 * ROWS, width), vm(PAIRS, PEERS, 2 * ROWS, width),
+        vm(tokens * n, LANES), vm(tokens * n, LANES), vb(SUB, 2 * blk), vb(2 * SUB, 2 * blk),
+        vm(PAIRS, 2, ENDS, width), vm(PAIRS, PEERS, ENDS, width),
     ] + [vm(tokens, width)] * 5 + [vm((tokens + 1) * n, width), vm(tokens * n, width)] + [
-        vb(blk, width), vb(blk, width), vb(2 * blk, width), vb(2 * blk, width), vb(blk, width), vb(blk, width),
-        vm(rows16, width), vm(rows16, width), vm(rows16, width), vm(tokens * n, LANES), vm(tokens * n, LANES),
+        ] + [vb(2 * blk, width)] * 6 + [
+        vm(rows16 + 2 * SUB, width), vm(rows16, width), vm(rows16 + 2 * SUB, width), vm(tokens * n, LANES), vm(tokens * n, LANES),
         vm(2, rank, width), vm(2, rank, width), vm(2, ROWS, width), vm(2, ROWS, width),
         vb(2, rank, width), vm(2, ROWS, width), vb(PAIRS - 1, rank, width), vm(PAIRS - 1, ROWS, width),
-        vm(rank, width), vm(ROWS, width), vm(8, rank // 8, width), vm(8, ROWS, width), vm(rank, width),
+        vm(rank, width), vm(ROWS, width), vb(rank, width), vb(8, rank // 8, width), vm(8, ROWS, width), vm(rank, width),
     ] + [dma(PAIRS)] * 8 + [dma(PAIRS, PEERS)] * 2 + [dma(PAIRS)] * 8 + [dma(PEERS)] * 6 + [dma(2, 2)] * 2 + [
         pltpu.SemaphoreType.DMA, pltpu.SemaphoreType.DMA, dma(5), pltpu.SemaphoreType.REGULAR]
     points = tokens * n * chans

time: 238 us -> 217 us (0.912)
  Pallas kernels: 226 us -> 206 us
    pallas_call x1, Pallas kernels: 226 us -> 206 us  [run(): pl.pallas_call(kernel, in_specs=[vmem] * 5 + [hbm] * 3 + [vmem] * 3, out_...]
where the time goes in v4:
time: 217 us; the launch traced here: 216 us
  Pallas kernels  206 us (95%)
  local copies, waits for them, and re-layouts  9.24 us (4%)
    pallas_call x1, Pallas kernels, run(): pl.pallas_call(kernel, in_specs=[vmem] * 5 + [hbm] * 3 + [vmem] * 3, out_...  206 us
    unnamed x25, local copies, waits for them, and re-layouts  9.24 us

profile of v4, /device:TPU:4, one launch (start us, length us, event | category | flops | bytes accessed | tf_op | source)
XLA Modules:
  0.0 215.8 jit_solution(14606401113702172440)
XLA Ops:
  0.6 205.9 %scan_backward.1 = (bf16[128,8192]{1,0:T(8,128)(2,1)}, bf16[128,8192]{1,0:T(8,128)(2,1)}, f32[128,512]{1,0:T(8,128)}, f32[16,128]{1,0:T(8,128)}, f32[16,128]{1,0...) custom-call(bf16[128,512]{1,0:T(8,128)(2,1)} %bitcast.25, ...), custom_call_target="tpu_custom_call" | custom-call | flops 503316480 | bytes 20971520 | tf_op jit(solution)/shard_map/scan_backward/pallas_call | solution.py:523
  206.5 0.0 copy-start
  206.5 3.2 %copy.29 = bf16[1,128,8192]{2,1,0:T(8,128)(2,1)} copy(bf16[1,128,8192]{2,1,0:T(8,128)(2,1)} %bitcast.16) | data formatting | bytes 4194304
  209.8 0.0 copy-done
  209.8 0.0 copy-start.2
  209.8 0.0 copy-start.5
  209.8 0.0 copy-start.4
  209.8 0.0 copy-start.1
  209.8 1.3 copy.30
  211.1 0.0 copy-done.2
  211.1 0.0 copy-start.3
  211.1 0.0 copy-start.7
  211.1 0.0 copy-start.6
  211.1 0.7 copy.31
  211.8 0.0 copy-done.5
  211.8 0.6 copy.32
  212.4 0.0 copy-done.4
  212.4 0.6 copy.33
  213.0 0.0 copy-done.1
  213.0 1.0 copy.34
  214.0 0.0 copy-done.3
  214.0 0.6 copy.35
  214.6 0.0 copy-done.7
  214.6 0.6 copy.36
  215.2 0.0 copy-done.6
  215.2 0.6 copy.37
Async XLA Ops:
  206.5 3.3 %copy-start = (bf16[128,8192]{1,0:T(8,128)(2,1)S(1)}, bf16[128,8192]{1,0:T(8,128)(2,1)}, u32[]{:S(2)}) copy-start(bf16[128,8192]{1,0:T(8,128)(2,1)} %get-tuple-element.19) | copy-start | bytes 6291460
  209.8 1.3 copy-start.2
  209.8 2.1 copy-start.5
  209.8 2.7 %copy-start.4 = (f32[16,128]{1,0:T(8,128)S(1)}, f32[16,128]{1,0:T(8,128)}, u32[]{:S(2)}) copy-start(f32[16,128]{1,0:T(8,128)} %get-tuple-element.22) | copy-start | bytes 24580
  209.8 3.3 %copy-start.1 = (f32[512,512]{1,0:T(8,128)S(1)}, f32[512,512]{1,0:T(8,128)}, u32[]{:S(2)}) copy-start(f32[512,512]{1,0:T(8,128)} %get-tuple-element.41) | copy-start | bytes 3145732
  211.1 2.9 %copy-start.3 = (f32[16,512]{1,0:T(8,128)S(1)}, f32[16,512]{1,0:T(8,128)}, u32[]{:S(2)}) copy-start(f32[16,512]{1,0:T(8,128)} %get-tuple-element.42) | copy-start | bytes 98308
  211.1 3.5 %copy-start.7 = (f32[1,512]{1,0:T(1,128)S(1)}, f32[1,512]{1,0:T(1,128)}, u32[]{:S(2)}) copy-start(f32[1,512]{1,0:T(1,128)} %get-tuple-element.25) | copy-start | bytes 6148
  211.1 4.1 %copy-start.6 = (f32[1,512]{1,0:T(1,128)S(1)}, f32[1,512]{1,0:T(1,128)}, u32[]{:S(2)}) copy-start(f32[1,512]{1,0:T(1,128)} %get-tuple-element.26) | copy-start | bytes 6148
